TPU v7x, 32 devices: a whole 2x2x4 slice. The times are simulated.
32 devices in a mesh: ctx: 8 (over z, x), head: 4 (over y, core).
Axes of the slice: x: 2, y: 2, z: 4, core: 2. Of those that a mesh axis runs over, the one named last changes fastest.
Arguments:
- queries: bfloat16 [8192, 4, 4, 128], P('ctx', None, 'head'), may hold values from -4.5 to 4.5
- key_rows: bfloat16 [8192, 4, 128], P('ctx'), may hold values from -3 to 3
- value_rows: bfloat16 [8192, 4, 128], P('ctx'), may hold values from -6 to 6
- out_grad: bfloat16 [8192, 4, 4, 128], P('ctx', None, 'head'), may hold values from -18 to 18
- outputs: bfloat16 [8192, 4, 4, 128], P('ctx', None, 'head'), may hold values from -6 to 6
- logsumexp: float32 [4, 4, 8192], P(None, 'head', 'ctx')
- selections: int32 [64, 3], P('ctx'), may hold values from 0 to 7, as said below
Outputs:
- grad_queries: bfloat16 [8192, 4, 4, 128], P('ctx', None, 'head')
- grad_keys: bfloat16 [8192, 4, 128], P('ctx', 'head')
- grad_values: bfloat16 [8192, 4, 128], P('ctx', 'head')
Inputs may be any that keep to these rules, and one draw needn't show every extreme that they name: `selections`: column 0 of row b is the query block's own key block b // 8; columns 1 and 2 each name an earlier key block or repeat the own block, and two earlier blocks in one row differ. The query blocks of one key block never name the same earlier block twice. For every key block after the first, exactly one of its query blocks names key block 0.
All inputs are finite; a program needn't handle non-finite values.
Results may differ from a plain program's by a relative error of at most 0.005.
Values may be sent and summed in bfloat16 or wider, within the bound.
A program may use at most 128 MiB of HBM per device.

v0:
```python
import jax
import jax.numpy as jnp
from jax import lax
from jax.sharding import PartitionSpec as P

QB = 128


def slot_grads(
    query_part, grad_part, lse_part, delta_part, weight, key_part, value_part, causal, scale
):
    scores = (
        jnp.einsum("srkgd,ckd->skgrc", query_part, key_part, preferred_element_type=jnp.float32)
        * scale
    )
    live = weight[:, None, None, None, None] > 0
    if causal is not None:
        live = live & causal
    prob = jnp.where(live, jnp.exp(scores - lse_part[..., None]), 0.0)
    dprob = jnp.einsum(
        "srkgd,ckd->skgrc", grad_part, value_part, preferred_element_type=jnp.float32
    )
    dscore = prob * (dprob - delta_part[..., None])
    prob_low = prob.astype(jnp.bfloat16)
    dscore_low = dscore.astype(jnp.bfloat16)
    grad_q = (
        jnp.einsum("skgrc,ckd->srkgd", dscore_low, key_part, preferred_element_type=jnp.float32)
        * scale
    )
    grad_k = (
        jnp.einsum("skgrc,srkgd->ckd", dscore_low, query_part, preferred_element_type=jnp.float32)
        * scale
    )
    grad_v = jnp.einsum("skgrc,srkgd->ckd", prob_low, grad_part, preferred_element_type=jnp.float32)
    return (grad_q, grad_k, grad_v)


def body(queries, key_rows, value_rows, out_grad, outputs, logsumexp, selections):
    row_count, kv_heads, local_heads, head_dim = queries.shape
    width = local_heads * head_dim
    block_count = row_count // QB
    peers = lax.axis_size("ctx")
    device = lax.axis_index("ctx")
    scale = head_dim ** (-0.5)
    delta_local = jnp.transpose(
        jnp.sum(out_grad.astype(jnp.float32) * outputs.astype(jnp.float32), axis=-1), (1, 2, 0)
    )
    causal = jnp.arange(row_count)[:, None] >= jnp.arange(row_count)[None, :]
    own_q, grad_k, grad_v = slot_grads(
        queries[None],
        out_grad[None],
        logsumexp[None],
        delta_local[None],
        jnp.ones((1,), jnp.float32),
        key_rows,
        value_rows,
        causal,
        scale,
    )
    grad_total = own_q.reshape(block_count, QB, kv_heads, width)
    block_ids = jnp.arange(block_count, dtype=jnp.int32)
    peer_ids = jnp.arange(peers, dtype=jnp.int32)
    remote = selections[:, 1:]
    match = jnp.any(remote[:, :, None] == peer_ids[None, None, :], axis=1) & (
        peer_ids[None, :] != device
    )
    lse_blocks = logsumexp.reshape(kv_heads, local_heads, block_count, QB)
    delta_blocks = delta_local.reshape(kv_heads, local_heads, block_count, QB)
    match_f = match.astype(jnp.float32)
    flag_send = jnp.sum(match_f, axis=0)
    source = jnp.sum(jnp.where(match, block_ids[:, None], 0), axis=0)
    send_q = jnp.take(queries.reshape(block_count, QB, kv_heads, width), source, axis=0)
    send_g = jnp.take(out_grad.reshape(block_count, QB, kv_heads, width), source, axis=0)
    send_lse = jnp.transpose(jnp.take(lse_blocks, source, axis=2), (2, 0, 1, 3))
    send_delta = jnp.transpose(jnp.take(delta_blocks, source, axis=2), (2, 0, 1, 3))
    recv_lse, recv_delta, recv_flag = (
        lax.all_to_all(send_lse, "ctx", split_axis=0, concat_axis=0, tiled=True),
        lax.all_to_all(send_delta, "ctx", split_axis=0, concat_axis=0, tiled=True),
        lax.all_to_all(flag_send, "ctx", split_axis=0, concat_axis=0, tiled=True),
    )
    recv_q, recv_g = (
        lax.all_to_all(send_q, "ctx", split_axis=0, concat_axis=0, tiled=True),
        lax.all_to_all(send_g, "ctx", split_axis=0, concat_axis=0, tiled=True),
    )
    ordering = jnp.argsort((recv_flag <= 0).astype(jnp.int32) * peers + peer_ids)
    sorted_q = jnp.take(recv_q, ordering, axis=0).reshape(
        peers, QB, kv_heads, local_heads, head_dim
    )
    sorted_g = jnp.take(recv_g, ordering, axis=0).reshape(
        peers, QB, kv_heads, local_heads, head_dim
    )
    sorted_lse = jnp.take(recv_lse, ordering, axis=0)
    sorted_delta = jnp.take(recv_delta, ordering, axis=0)
    sorted_flag = jnp.take(recv_flag, ordering, axis=0)
    group_size = 4
    empty_q = jnp.zeros((group_size, QB, kv_heads, local_heads, head_dim), jnp.float32)

    def group_step(group_turn, carry):
        dq_slots, acc_k, acc_v = carry
        start = group_turn * group_size
        part_flag = lax.dynamic_slice_in_dim(sorted_flag, start, group_size, 0)
        part_q = lax.dynamic_slice_in_dim(sorted_q, start, group_size, 0)
        part_g = lax.dynamic_slice_in_dim(sorted_g, start, group_size, 0)
        part_lse = lax.dynamic_slice_in_dim(sorted_lse, start, group_size, 0)
        part_delta = lax.dynamic_slice_in_dim(sorted_delta, start, group_size, 0)

        def active(unused):
            return slot_grads(
                part_q, part_g, part_lse, part_delta, part_flag, key_rows, value_rows, None, scale
            )

        def skipped(unused):
            return (empty_q, jnp.zeros_like(acc_k), jnp.zeros_like(acc_v))

        group_q, group_k, group_v = lax.cond(jnp.sum(part_flag) > 0, active, skipped, None)
        dq_slots = lax.dynamic_update_slice_in_dim(dq_slots, group_q, start, 0)
        return (dq_slots, acc_k + group_k, acc_v + group_v)

    dq_init = jnp.zeros((peers, QB, kv_heads, local_heads, head_dim), jnp.float32)
    dq_sorted, grad_k, grad_v = lax.fori_loop(
        0, peers // group_size, group_step, (dq_init, grad_k, grad_v)
    )
    restore = jnp.argsort(ordering)
    dq_back = jnp.take(dq_sorted, restore, axis=0).reshape(peers, QB, kv_heads, width)
    returned = lax.all_to_all(dq_back, "ctx", split_axis=0, concat_axis=0, tiled=True)
    grad_total = grad_total + jnp.einsum(
        "ip,pqke->iqke", match_f, returned, precision=lax.Precision.HIGHEST
    )
    shard_k, shard_v = (
        lax.psum_scatter(grad_k, "head", scatter_dimension=1, tiled=True),
        lax.psum_scatter(grad_v, "head", scatter_dimension=1, tiled=True),
    )
    grad_queries = grad_total.reshape(row_count, kv_heads, local_heads, head_dim).astype(
        jnp.bfloat16
    )
    return (grad_queries, shard_k.astype(jnp.bfloat16), shard_v.astype(jnp.bfloat16))


def solution(mesh):
    in_specs = (
        P("ctx", None, "head", None),
        P("ctx", None, None),
        P("ctx", None, None),
        P("ctx", None, "head", None),
        P("ctx", None, "head", None),
        P(None, "head", "ctx"),
        P("ctx", None),
    )
    out_specs = (P("ctx", None, "head", None), P("ctx", "head", None), P("ctx", "head", None))
    return jax.shard_map(body, mesh=mesh, in_specs=in_specs, out_specs=out_specs, check_vma=False)
```

profile of v0, /device:TPU:1, one launch (start us, length us, event | category | flops | bytes accessed | tf_op | source)
XLA Modules:
  0.0 222.6 jit_solution(3458609809333389389)
XLA Ops:
  8.7 6.4 %all-to-all-start = ((f32[8,1,1]{2,1,0:T(1,128)}), f32[8,1,1]{2,1,0:T(1,128)S(1)}, u32[]{:S(2)}, u32[]{:S(2)}) async-start(f32[8,1,1]{2,1,0:T(1,128)} %copy.171), calls=%async_computation | async-start | bytes 8192 | tf_op jit(solution)/shard_map/all_to_all | solution.py:79
  15.2 2.7 %multiply_reduce_fusion = f32[1024,4]{1,0:T(8,128)S(1)} fusion(bf16[1024,4,1,128]{3,1,2,0:T(4,128)(2,1)} %param.21, bf16[1024,4,1,128]{3,1,2,0:T(4,128)(2,1)} %param.20), kind=kLoop, calls=%fused_computation.71 | loop fusion | flops 2093056 | bytes 2113536 | tf_op jit(solution)/shard_map/reduce_sum | solution.py:46
  20.7 5.4 %all-to-all-start.4 = ((f32[8,4,1,128]{3,1,2,0:T(4,128)}), f32[8,4,1,128]{3,1,2,0:T(4,128)S(1)}, u32[]{:S(2)}, u32[]{:S(2)}) async-start(f32[8,4,1,128]{3,1,2,0:T(4,128)} %get-tuple-element.402), calls=%async_computation.4 | async-start | bytes 32768 | tf_op jit(solution)/shard_map/all_to_all | solution.py:78
  26.1 2.5 %copy.179 = bf16[8,128,4,128]{3,1,2,0:T(8,128)(2,1)} copy(bf16[8,128,4,128]{3,2,1,0:T(4,128)(2,1)} %bitcast.208) | data formatting | bytes 2097152 | tf_op jit(solution)/shard_map/reshape | solution.py:73
  33.8 5.4 %all-to-all-start.2 = ((f32[8,4,1,128]{3,1,2,0:T(4,128)}), f32[8,4,1,128]{3,1,2,0:T(4,128)S(1)}, u32[]{:S(2)}, u32[]{:S(2)}) async-start(f32[8,4,1,128]{3,1,2,0:T(4,128)} %get-tuple-element.403), calls=%async_computation.2 | async-start | bytes 32768 | tf_op jit(solution)/shard_map/all_to_all | solution.py:77
  40.9 3.8 %all-to-all-done.2 = f32[8,4,1,128]{3,1,2,0:T(4,128)S(1)} async-done(((f32[8,4,1,128]{3,1,2,0:T(4,128)}), f32[8,4,1,128]{3,1,2,0:T(4,128)S(1)}, u32[]{:S(2)}, u32[]{:S(2)}) %all-to-all-start.2) | async-done | bytes 16416 | tf_op jit(solution)/shard_map/all_to_all | solution.py:77
  44.7 3.6 %all-to-all-start.3 = ((bf16[8,128,4,128]{3,1,2,0:T(8,128)(2,1)}), bf16[8,128,4,128]{3,1,2,0:T(8,128)(2,1)S(1)}, u32[]{:S(2)}, u32[]{:S(2)}) async-start(bf16[8,128,4,128]{3,1,2,0:T(8,128)(2,1)} %get-tuple-element.406), calls=%async_computation.3 | async-start | bytes 2097152 | tf_op jit(solution)/shard_map/all_to_all | solution.py:83
  48.2 9.7 %fusion.63 = f32[4,1024,1024]{2,1,0:T(8,128)} fusion(bf16[1024,4,128]{2,1,0:T(4,128)(2,1)} %bitcast.205, bf16[1024,4,128]{2,1,0:T(4,128)(2,1)} %param.18), kind=kOutput, calls=%fused_computation.82 | convolution fusion | flops 1073741824 | bytes 18874368 | tf_op jit(solution)/shard_map/srkgd,ckd->skgrc/dot_general | solution.py:13
  59.5 11.7 %fusion.36 = bf16[1,4,1,1024,1024]{3,4,1,2,0:T(8,128)(2,1)} fusion(f32[4,1024,1024]{2,1,0:T(8,128)} %fusion.63, f32[4,1024]{1,0:T(4,128)S(1)} %copy.168, f32[4,1024]{1,0:T(4,128)S(1)} %bitcast.218, pred[1024,1024]{0,1:T(8,128)(4,1)S(1)} %iota_compare_fusion, bf16[1024,4,128]{2,1,0:T(4,128)(2,1)S(1)} %bitcast.210, bf16[1024,4,128]{2,1,0:T(4,128)(2,1)} %param.19), kind=kOutput, calls=%fused_computation.52 | convolution fusion | flops 1098907648 | bytes 28344320 | tf_op jit(solution)/shard_map/srkgd,ckd->skgrc/dot_general | solution.py:20
  72.0 4.9 %all-to-all-start.1 = ((bf16[8,128,4,128]{3,1,2,0:T(8,128)(2,1)}), bf16[8,128,4,128]{3,1,2,0:T(8,128)(2,1)}, u32[]{:S(2)}, u32[]{:S(2)}) async-start(bf16[8,128,4,128]{3,1,2,0:T(8,128)(2,1)} %get-tuple-element.407), calls=%async_computation.1 | async-start | bytes 2097152 | tf_op jit(solution)/shard_map/all_to_all | solution.py:82
  77.1 10.9 %fusion.50 = f32[1024,4,128]{2,0,1:T(8,128)} fusion(f32[4,1024,1024]{2,1,0:T(8,128)} %fusion.63, f32[4,1024]{1,0:T(4,128)S(1)} %bitcast.219, pred[1024,1024]{0,1:T(8,128)(4,1)} %copy-done.9, bf16[1024,4,128]{2,1,0:T(4,128)(2,1)} %bitcast.209), kind=kOutput, calls=%fused_computation.72 | convolution fusion | flops 1090519040 | bytes 20987904 | tf_op jit(solution)/shard_map/skgrc,srkgd->ckd/dot_general | solution.py:34
  89.2 2.4 %copy.166 = bf16[1024,4,128]{2,0,1:T(8,128)(2,1)} copy(bf16[1024,4,128]{2,1,0:T(4,128)(2,1)} %param.19) | data formatting | bytes 2097152 | tf_op args[2]
  91.5 7.0 %multiply_bitcast_fusion = f32[1024,4,128]{2,0,1:T(8,128)} fusion(bf16[1,4,1,1024,1024]{3,4,1,2,0:T(8,128)(2,1)} %fusion.36, bf16[1024,4,128]{2,1,0:T(4,128)(2,1)S(1)} %bitcast.207), kind=kOutput, calls=%fused_computation.70 | convolution fusion | flops 1074266112 | bytes 11534336 | tf_op jit(solution)/shard_map/skgrc,srkgd->ckd/dot_general | solution.py:31
  108.3 38.7 %while.17 = (s32[]{:T(128)}, f32[8,128,4,1,128]{4,1,2,0,3:T(8,128)}, f32[1024,4,128]{2,0,1:T(8,128)}, f32[1024,4,128]{2,0,1:T(8,128)}, f32[8]{0:T(128)S(1)}, /*i...) while((s32[]{:T(128)}, ...), condition=%wide.region_10.14_spmd, body=%wide.region_6.13_spmd.sunk | while | flops 2707161088 | bytes 79751656 | solution.py:120
  109.5 10.8 %conditional.2 = (f32[4,128,4,1,128]{4,1,0,2,3:T(8,128)S(1)}, f32[1024,4,128]{2,0,1:T(8,128)S(1)}, f32[1024,4,128]{2,0,1:T(8,128)S(1)}) conditional(s32[]{:T(128)} %convert_element_type.83, () %tuple.71, (f32[4]{0:T(128)S(1)}, bf16[8,128,4,1,128]{4,1,0,2,3:T(8,128)(2,1)}, s32[]{:T(128)}, bf16[1024,4,128]{2,0,1:T(8,128)(2,1)}, ...), branch_computations={%region_8.11_spmd, %region_9.12_spmd} | conditional | flops 2706112512 | bytes 65070764 | solution.py:115
  109.6 2.8 %fusion.20 = f32[4,4,128,1024]{3,2,1,0:T(8,128)S(1)} fusion(bf16[1024,4,128]{2,0,1:T(8,128)(2,1)} %get-tuple-element.244, bf16[8,128,4,1,128]{4,1,0,2,3:T(8,128)(2,1)} %get-tuple-element.242, s32[]{:T(128)} %get-tuple-element.243), kind=kOutput, calls=%fused_computation.31 | convolution fusion | flops 536870912 | bytes 9961984 | tf_op jit(solution)/shard_map/while/body/eval_jaxpr/cond/branch_1_fun/srkgd,ckd->skgrc/dot_general | solution.py:13
  112.4 2.5 %fusion.8 = bf16[4,4,128,1024]{3,2,0,1:T(8,128)(2,1)S(1)} fusion(f32[4,4,128,1024]{3,2,1,0:T(8,128)S(1)} %fusion.20, f32[4,4,128]{2,0,1:T(4,128)S(1)} %get-tuple-element.398, f32[4,4,128]{2,0,1:T(4,128)S(1)} %get-tuple-element.399, pred[4]{0:T(512)(128)(4,1)S(1)} %broadcast_compare_fusion, bf16[1024,4,128]{2,0,1:T(8,128)(2,1)S(1)} %copy-done.7, ...), kind=kOutput, calls=%fused_computation.19 | convolution fusion | flops 549453824 | bytes 14172676 | tf_op jit(solution)/shard_map/while/body/eval_jaxpr/cond/branch_1_fun/srkgd,ckd->skgrc/dot_general | solution.py:20
  117.9 2.4 %fusion.14 = f32[1024,4,128]{2,0,1:T(8,128)S(1)} fusion(f32[4,4,128,1024]{3,2,1,0:T(8,128)S(1)} %fusion.20, f32[4,4,128]{2,0,1:T(4,128)S(1)} %get-tuple-element.399, pred[4]{0:T(512)(128)(4,1)S(1)} %broadcast_compare_fusion, bf16[8,128,4,1,128]{4,1,0,2,3:T(8,128)(2,1)S(1)} %copy-done.8, s32[]{:T(128)} %get-tuple-element.243), kind=kOutput, calls=%fused_computation.26 | convolution fusion | flops 545259520 | bytes 11018756 | tf_op jit(solution)/shard_map/while/body/eval_jaxpr/cond/branch_1_fun/skgrc,srkgd->ckd/dot_general | solution.py:34
  121.4 3.1 %add.107 = f32[1024,4,128]{2,0,1:T(8,128)} add(f32[1024,4,128]{2,0,1:T(8,128)} %get-tuple-element.509, f32[1024,4,128]{2,0,1:T(8,128)S(1)} %get-tuple-element.483) | non-fusion elementwise | flops 524288 | bytes 6291456 | tf_op jit(solution)/shard_map/while/body/eval_jaxpr/add | solution.py:117
  124.5 3.2 %add.108 = f32[1024,4,128]{2,0,1:T(8,128)} add(f32[1024,4,128]{2,0,1:T(8,128)} %get-tuple-element.510, f32[1024,4,128]{2,0,1:T(8,128)S(1)} %get-tuple-element.484) | non-fusion elementwise | flops 524288 | bytes 6291456 | tf_op jit(solution)/shard_map/while/body/eval_jaxpr/add | solution.py:117
  128.9 10.8 %conditional.2 = (f32[4,128,4,1,128]{4,1,0,2,3:T(8,128)S(1)}, f32[1024,4,128]{2,0,1:T(8,128)S(1)}, f32[1024,4,128]{2,0,1:T(8,128)S(1)}) conditional(s32[]{:T(128)} %convert_element_type.83, () %tuple.71, (f32[4]{0:T(128)S(1)}, bf16[8,128,4,1,128]{4,1,0,2,3:T(8,128)(2,1)}, s32[]{:T(128)}, bf16[1024,4,128]{2,0,1:T(8,128)(2,1)}, ...), branch_computations={%region_8.11_spmd, %region_9.12_spmd} | conditional | flops 2706112512 | bytes 65070764 | solution.py:115
  128.9 2.8 %fusion.20 = f32[4,4,128,1024]{3,2,1,0:T(8,128)S(1)} fusion(bf16[1024,4,128]{2,0,1:T(8,128)(2,1)} %get-tuple-element.244, bf16[8,128,4,1,128]{4,1,0,2,3:T(8,128)(2,1)} %get-tuple-element.242, s32[]{:T(128)} %get-tuple-element.243), kind=kOutput, calls=%fused_computation.31 | convolution fusion | flops 536870912 | bytes 9961984 | tf_op jit(solution)/shard_map/while/body/eval_jaxpr/cond/branch_1_fun/srkgd,ckd->skgrc/dot_general | solution.py:13
  131.8 2.5 %fusion.8 = bf16[4,4,128,1024]{3,2,0,1:T(8,128)(2,1)S(1)} fusion(f32[4,4,128,1024]{3,2,1,0:T(8,128)S(1)} %fusion.20, f32[4,4,128]{2,0,1:T(4,128)S(1)} %get-tuple-element.398, f32[4,4,128]{2,0,1:T(4,128)S(1)} %get-tuple-element.399, pred[4]{0:T(512)(128)(4,1)S(1)} %broadcast_compare_fusion, bf16[1024,4,128]{2,0,1:T(8,128)(2,1)S(1)} %copy-done.7, ...), kind=kOutput, calls=%fused_computation.19 | convolution fusion | flops 549453824 | bytes 14172676 | tf_op jit(solution)/shard_map/while/body/eval_jaxpr/cond/branch_1_fun/srkgd,ckd->skgrc/dot_general | solution.py:20
  137.2 2.4 %fusion.14 = f32[1024,4,128]{2,0,1:T(8,128)S(1)} fusion(f32[4,4,128,1024]{3,2,1,0:T(8,128)S(1)} %fusion.20, f32[4,4,128]{2,0,1:T(4,128)S(1)} %get-tuple-element.399, pred[4]{0:T(512)(128)(4,1)S(1)} %broadcast_compare_fusion, bf16[8,128,4,1,128]{4,1,0,2,3:T(8,128)(2,1)S(1)} %copy-done.8, s32[]{:T(128)} %get-tuple-element.243), kind=kOutput, calls=%fused_computation.26 | convolution fusion | flops 545259520 | bytes 11018756 | tf_op jit(solution)/shard_map/while/body/eval_jaxpr/cond/branch_1_fun/skgrc,srkgd->ckd/dot_general | solution.py:34
  140.7 3.1 %add.107 = f32[1024,4,128]{2,0,1:T(8,128)} add(f32[1024,4,128]{2,0,1:T(8,128)} %get-tuple-element.509, f32[1024,4,128]{2,0,1:T(8,128)S(1)} %get-tuple-element.483) | non-fusion elementwise | flops 524288 | bytes 6291456 | tf_op jit(solution)/shard_map/while/body/eval_jaxpr/add | solution.py:117
  143.8 3.2 %add.108 = f32[1024,4,128]{2,0,1:T(8,128)} add(f32[1024,4,128]{2,0,1:T(8,128)} %get-tuple-element.510, f32[1024,4,128]{2,0,1:T(8,128)S(1)} %get-tuple-element.484) | non-fusion elementwise | flops 524288 | bytes 6291456 | tf_op jit(solution)/shard_map/while/body/eval_jaxpr/add | solution.py:117
  150.7 2.7 %copy.190 = f32[8,128,4,128]{3,2,1,0:T(4,128)} copy(f32[8,128,4,128]{3,1,2,0:T(8,128)S(1)} %broadcast_select_fusion) | data formatting | bytes 4194304 | tf_op jit(solution)/shard_map/jit(_take)/select_n | solution.py:124
  153.3 3.9 %all-to-all-start.5 = ((f32[8,128,4,128]{3,2,1,0:T(4,128)}), f32[8,128,4,128]{3,2,1,0:T(4,128)S(1)}, u32[]{:S(2)}, u32[]{:S(2)}) async-start(f32[8,128,4,128]{3,2,1,0:T(4,128)} %copy.190), calls=%async_computation.5 | async-start | bytes 4194304 | tf_op jit(solution)/shard_map/all_to_all | solution.py:125
  157.2 7.8 %fusion.53 = f32[4,1024,128]{2,1,0:T(8,128)} fusion(bf16[1,4,1,1024,1024]{3,4,1,2,0:T(8,128)(2,1)} %fusion.36, bf16[1024,4,128]{2,1,0:T(4,128)(2,1)S(1)} %copy-done.5), kind=kOutput, calls=%fused_computation.73 | convolution fusion | flops 1074266112 | bytes 11534336 | tf_op jit(solution)/shard_map/skgrc,ckd->srkgd/dot_general | solution.py:27
  165.0 36.5 %all-to-all-done.5 = f32[8,128,4,128]{3,2,1,0:T(4,128)S(1)} async-done(((f32[8,128,4,128]{3,2,1,0:T(4,128)}), f32[8,128,4,128]{3,2,1,0:T(4,128)S(1)}, u32[]{:S(2)}, u32[]{:S(2)}) %all-to-all-start.5) | async-done | bytes 2097184 | tf_op jit(solution)/shard_map/all_to_all | solution.py:125
  201.5 5.1 %fusion.47 = bf16[8,128,4,128]{3,0,2,1:T(8,128)(2,1)S(1)} fusion(f32[8,128,4,128]{3,1,0,2:T(8,128)} %bitcast.212, f32[8,128,4,128]{3,2,1,0:T(4,128)S(1)} %all-to-all-done.5, pred[8,8]{1,0:T(8,128)(4,1)S(1)} %copy-done.12, pred[8]{0:T(512)(128)(4,1)S(1)} %copy-done.14), kind=kOutput, calls=%fused_computation.67 | convolution fusion | flops 51380288 | bytes 5242952 | tf_op jit(solution)/shard_map/ip,pqke->iqke/dot_general | solution.py:126
  210.6 3.4 %reduce-scatter.5.cloned.1.call-done = f32[1024,1,128]{2,0,1:T(8,128)} async-done(((f32[1024,4,128]{2,0,1:T(8,128)}), f32[1024,1,128]{2,0,1:T(8,128)}) %reduce-scatter.5.cloned.1.call-update) | async-done | bytes 524304 | tf_op jit(solution)/shard_map/reduce_scatter | solution.py:131
  (111 shorter events, 43.2 us)
Async XLA Ops:
  7.2 23.4 %copy-start.2 = (bf16[1024,4,1,128]{3,1,2,0:T(4,128)(2,1)S(1)}, bf16[1024,4,1,128]{3,1,2,0:T(4,128)(2,1)}, u32[]{:S(2)}) copy-start(bf16[1024,4,1,128]{3,1,2,0:T(4,128)(2,1)} %param.17) | copy-start | bytes 3145732
  8.0 7.1 %copy-start.11 = (pred[8,8]{1,0:T(8,128)(4,1)}, pred[8,8]{1,0:T(8,128)(4,1)S(1)}, u32[]{:S(2)}) copy-start(pred[8,8]{1,0:T(8,128)(4,1)S(1)} %fusion.67) | copy-start | bytes 196
  8.0 23.7 %copy-start.13 = (pred[8]{0:T(512)(128)(4,1)}, pred[8]{0:T(512)(128)(4,1)S(1)}, u32[]{:S(2)}) copy-start(pred[8]{0:T(512)(128)(4,1)S(1)} %iota_compare_fusion.2) | copy-start | bytes 28
  8.7 11.9 %all-to-all-start = ((f32[8,1,1]{2,1,0:T(1,128)}), f32[8,1,1]{2,1,0:T(1,128)S(1)}, u32[]{:S(2)}, u32[]{:S(2)}) async-start(f32[8,1,1]{2,1,0:T(1,128)} %copy.171), calls=%async_computation | async-start | bytes 8192 | tf_op jit(solution)/shard_map/all_to_all | solution.py:79
  20.7 13.1 %all-to-all-start.4 = ((f32[8,4,1,128]{3,1,2,0:T(4,128)}), f32[8,4,1,128]{3,1,2,0:T(4,128)S(1)}, u32[]{:S(2)}, u32[]{:S(2)}) async-start(f32[8,4,1,128]{3,1,2,0:T(4,128)} %get-tuple-element.402), calls=%async_computation.4 | async-start | bytes 32768 | tf_op jit(solution)/shard_map/all_to_all | solution.py:78
  33.8 10.9 %all-to-all-start.2 = ((f32[8,4,1,128]{3,1,2,0:T(4,128)}), f32[8,4,1,128]{3,1,2,0:T(4,128)S(1)}, u32[]{:S(2)}, u32[]{:S(2)}) async-start(f32[8,4,1,128]{3,1,2,0:T(4,128)} %get-tuple-element.403), calls=%async_computation.2 | async-start | bytes 32768 | tf_op jit(solution)/shard_map/all_to_all | solution.py:77
  44.7 27.3 %all-to-all-start.3 = ((bf16[8,128,4,128]{3,1,2,0:T(8,128)(2,1)}), bf16[8,128,4,128]{3,1,2,0:T(8,128)(2,1)S(1)}, u32[]{:S(2)}, u32[]{:S(2)}) async-start(bf16[8,128,4,128]{3,1,2,0:T(8,128)(2,1)} %get-tuple-element.406), calls=%async_computation.3 | async-start | bytes 2097152 | tf_op jit(solution)/shard_map/all_to_all | solution.py:83
  48.2 9.7 %copy-start.10 = (f32[4,1,1024]{2,1,0:T(1,128)S(1)}, f32[4,1,1024]{2,1,0:T(1,128)}, u32[]{:S(2)}) copy-start(f32[4,1,1024]{2,1,0:T(1,128)} %param.22) | copy-start | bytes 49156
  48.2 11.2 %copy-start.6 = (bf16[1024,4,1,128]{3,1,2,0:T(4,128)(2,1)S(1)}, bf16[1024,4,1,128]{3,1,2,0:T(4,128)(2,1)}, u32[]{:S(2)}) copy-start(bf16[1024,4,1,128]{3,1,2,0:T(4,128)(2,1)} %param.20) | copy-start | bytes 3145732
  58.5 1.0 copy-start.9
  72.0 30.4 %all-to-all-start.1 = ((bf16[8,128,4,128]{3,1,2,0:T(8,128)(2,1)}), bf16[8,128,4,128]{3,1,2,0:T(8,128)(2,1)}, u32[]{:S(2)}, u32[]{:S(2)}) async-start(bf16[8,128,4,128]{3,1,2,0:T(8,128)(2,1)} %get-tuple-element.407), calls=%async_computation.1 | async-start | bytes 2097152 | tf_op jit(solution)/shard_map/all_to_all | solution.py:82
  76.9 11.2 %copy-start.4 = (bf16[1024,4,128]{2,1,0:T(4,128)(2,1)S(1)}, bf16[1024,4,128]{2,1,0:T(4,128)(2,1)}, u32[]{:S(2)}) copy-start(bf16[1024,4,128]{2,1,0:T(4,128)(2,1)} %param.18) | copy-start | bytes 3145732
  76.9 132.0 %reduce-scatter.3.cloned.1.call-start = ((), (), s32[]{:S(2)}) async-start(), calls=%async_computation.8 | async-start | bytes 2621440 | tf_op jit(solution)/shard_map/reduce_scatter | solution.py:130
  88.0 3.5 %copy-start.3 = (bf16[1024,4,1,128]{3,1,2,0:T(4,128)(2,1)S(1)}, bf16[1024,4,1,128]{3,1,2,0:T(4,128)(2,1)}, u32[]{:S(2)}) copy-start(bf16[1024,4,1,128]{3,1,2,0:T(4,128)(2,1)} %param.17) | copy-start | bytes 3145732
  109.5 2.8 %copy-start.7 = (bf16[1024,4,128]{2,0,1:T(8,128)(2,1)S(1)}, bf16[1024,4,128]{2,0,1:T(8,128)(2,1)}, u32[]{:S(2)}) copy-start(bf16[1024,4,128]{2,0,1:T(8,128)(2,1)} %get-tuple-element.247) | copy-start | bytes 3145732 | tf_op jit(solution)/shard_map/while/body/eval_jaxpr/cond
  109.5 2.8 %copy-start.8 = (bf16[8,128,4,1,128]{4,1,0,2,3:T(8,128)(2,1)S(1)}, bf16[8,128,4,1,128]{4,1,0,2,3:T(8,128)(2,1)}, u32[]{:S(2)}) copy-start(bf16[8,128,4,1,128]{4,1,0,2,3:T(8,128)(2,1)} %get-tuple-element.246) | copy-start | bytes 3145732 | tf_op jit(solution)/shard_map/while/body/eval_jaxpr/cond
  112.4 2.5 %copy-start = (bf16[1024,4,128]{2,0,1:T(8,128)(2,1)S(1)}, bf16[1024,4,128]{2,0,1:T(8,128)(2,1)}, u32[]{:S(2)}) copy-start(bf16[1024,4,128]{2,0,1:T(8,128)(2,1)} %get-tuple-element.244) | copy-start | bytes 3145732 | tf_op jit(solution)/shard_map/while/body/eval_jaxpr/cond
  114.9 1.3 copy-start.1
  128.9 2.8 %copy-start.7 = (bf16[1024,4,128]{2,0,1:T(8,128)(2,1)S(1)}, bf16[1024,4,128]{2,0,1:T(8,128)(2,1)}, u32[]{:S(2)}) copy-start(bf16[1024,4,128]{2,0,1:T(8,128)(2,1)} %get-tuple-element.247) | copy-start | bytes 3145732 | tf_op jit(solution)/shard_map/while/body/eval_jaxpr/cond
  128.9 2.8 %copy-start.8 = (bf16[8,128,4,1,128]{4,1,0,2,3:T(8,128)(2,1)S(1)}, bf16[8,128,4,1,128]{4,1,0,2,3:T(8,128)(2,1)}, u32[]{:S(2)}) copy-start(bf16[8,128,4,1,128]{4,1,0,2,3:T(8,128)(2,1)} %get-tuple-element.246) | copy-start | bytes 3145732 | tf_op jit(solution)/shard_map/while/body/eval_jaxpr/cond
  131.7 2.5 %copy-start = (bf16[1024,4,128]{2,0,1:T(8,128)(2,1)S(1)}, bf16[1024,4,128]{2,0,1:T(8,128)(2,1)}, u32[]{:S(2)}) copy-start(bf16[1024,4,128]{2,0,1:T(8,128)(2,1)} %get-tuple-element.244) | copy-start | bytes 3145732 | tf_op jit(solution)/shard_map/while/body/eval_jaxpr/cond
  134.3 1.3 copy-start.1
  147.0 67.0 %reduce-scatter.5.cloned.1.call-start = ((), (), s32[]{:S(2)}) async-start(), calls=%async_computation.9 | async-start | bytes 2621440 | tf_op jit(solution)/shard_map/reduce_scatter | solution.py:131
  150.6 6.6 %copy-start.5 = (bf16[1024,4,128]{2,1,0:T(4,128)(2,1)S(1)}, bf16[1024,4,128]{2,1,0:T(4,128)(2,1)}, u32[]{:S(2)}) copy-start(bf16[1024,4,128]{2,1,0:T(4,128)(2,1)} %param.18) | copy-start | bytes 3145732
  153.3 48.2 %all-to-all-start.5 = ((f32[8,128,4,128]{3,2,1,0:T(4,128)}), f32[8,128,4,128]{3,2,1,0:T(4,128)S(1)}, u32[]{:S(2)}, u32[]{:S(2)}) async-start(f32[8,128,4,128]{3,2,1,0:T(4,128)} %copy.190), calls=%async_computation.5 | async-start | bytes 4194304 | tf_op jit(solution)/shard_map/all_to_all | solution.py:125
  157.2 44.3 %copy-start.12 = (pred[8,8]{1,0:T(8,128)(4,1)S(1)}, pred[8,8]{1,0:T(8,128)(4,1)}, u32[]{:S(2)}) copy-start(pred[8,8]{1,0:T(8,128)(4,1)} %copy-done.11) | copy-start | bytes 196
  157.2 44.3 %copy-start.14 = (pred[8]{0:T(512)(128)(4,1)S(1)}, pred[8]{0:T(512)(128)(4,1)}, u32[]{:S(2)}) copy-start(pred[8]{0:T(512)(128)(4,1)} %copy-done.13) | copy-start | bytes 28
Sparse Core Ops, SparseCore 0:
  147.1 32.6 reduce-scatter.2
  182.5 31.4 reduce-scatter.4
where the time goes:
time: 225 us; the launch traced here: 223 us
  matrix products  73.5 us (33%)
  waiting for transfers between devices  44.5 us (20%)
  local copies, waits for them, and re-layouts  33.4 us (15%)
  starting transfers between devices  29.9 us (13%)
  other arithmetic  25.7 us (11%)
  between operations  14.3 us (6%)
    all_to_all x1, waiting for transfers between devices, body(): lax.all_to_all(dq_back, 'ctx', split_axis=0, concat_axis=0, tiled=True)  36.5 us
    dot_general x3, matrix products, slot_grads(): jnp.einsum('srkgd,ckd->skgrc', grad_part, value_part, preferred_element_t...  16.7 us
    dot_general x3, matrix products, slot_grads(): jnp.einsum('skgrc,srkgd->ckd', prob_low, grad_part, preferred_element_typ...  15.7 us
    dot_general x3, matrix products, slot_grads(): jnp.einsum('srkgd,ckd->skgrc', query_part, key_part, preferred_element_ty...  15.3 us
    add x4, other arithmetic, group_step(): return (dq_slots, acc_k + group_k, acc_v + group_v)  12.6 us
    dot_general x3, matrix products, slot_grads(): jnp.einsum('skgrc,srkgd->ckd', dscore_low, query_part, preferred_element_...  10.4 us
    dot_general x3, matrix products, slot_grads(): jnp.einsum('skgrc,ckd->srkgd', dscore_low, key_part, preferred_element_ty...  10.3 us
    all_to_all x1, starting transfers between devices, body(): lax.all_to_all(flag_send, 'ctx', split_axis=0, concat_axis=0, tiled=True)  6.35 us
  transfers between devices with their start and end apart: 8, of which 4 were waited for; matrix products, arithmetic and copies ran while one was open for 38% of the time, Pallas kernels for 0%

commit v1 on v0

v1 whole, which is shorter than its diff:
```python
import functools
import math

import jax
import jax.numpy as jnp
from jax import lax
from jax.experimental import pallas as pl
from jax.experimental.pallas import tpu as pltpu
from jax.sharding import PartitionSpec as P

QB = 128
TILE = 256
DEAD = 1e30
LOG2E = math.log2(math.e)
NT = (((1,), (1,)), ((), ()))
VMEM_LIMIT = 48 * 1024 * 1024


def dot(a, b, dims=(((1,), (0,)), ((), ()))):
    return lax.dot_general(a, b, dims, preferred_element_type=jnp.float32)


def piece(k, k_t, v, q, g, lse2, delta, scale, causal=False):
    p = jnp.exp2(dot(k, q, NT) * (scale * LOG2E) - lse2)
    if causal:
        keep = lax.broadcasted_iota(jnp.int32, p.shape, 0) <= lax.broadcasted_iota(
            jnp.int32, p.shape, 1
        )
        p = jnp.where(keep, p, 0.0)
    ds = (p * (dot(v, g, NT) - delta)).astype(jnp.bfloat16)
    return dot(k_t, ds), dot(ds, q), dot(p.astype(jnp.bfloat16), g)


def pick_kernel(source_ref, live_ref, q_ref, g_ref, stat_ref, q_out, g_out, stat_out):
    rows = stat_ref.shape[1]
    for peer in range(q_out.shape[0]):
        block = source_ref[peer]
        q_out[peer] = q_ref[block]
        g_out[peer] = g_ref[block]
        stat_out[peer, :rows] = stat_ref[block]
        live = live_ref[peer].astype(jnp.float32)
        stat_out[peer, rows:] = jnp.full((stat_out.shape[1] - rows, QB), live, jnp.float32)


def own_kernel(scale, q_ref, g_ref, k_ref, v_ref, lse_ref, delta_ref, dq_ref, dk_ref, dv_ref):
    rows = q_ref.shape[0]
    k_t = k_ref[...].T
    for lo in range(0, rows, TILE):
        here = pl.ds(lo, TILE)
        q, g = q_ref[here, :], g_ref[here, :]
        lse2, delta = lse_ref[0, :, here] * LOG2E, delta_ref[0, :, here]
        dq, dk, dv = piece(
            k_ref[here, :], k_t[:, lo : lo + TILE], v_ref[here, :], q, g, lse2, delta, scale, True
        )
        dk_ref[here, :] = dk
        dv_ref[here, :] = dv
        if lo:
            dq_more, dk, dv = piece(
                k_ref[:lo, :], k_t[:, :lo], v_ref[:lo, :], q, g, lse2, delta, scale
            )
            dq += dq_more
            dk_ref[:lo, :] += dk
            dv_ref[:lo, :] += dv
        dq_ref[here, :] = dq.T * scale


def slots_kernel(
    scale, mark_ref, q_ref, g_ref, stat_ref, k_ref, v_ref, dk_in, dv_in, dq_ref, dk_ref, dv_ref,
    acc_k, acc_v,
):
    head = pl.program_id(0)
    heads = pl.num_programs(0)
    k_t = k_ref[...].T
    acc_k[...] = dk_in[...]
    acc_v[...] = dv_in[...]
    for slot in range(q_ref.shape[0] // QB):
        here = pl.ds(slot * QB, QB)

        @pl.when(mark_ref[slot] > 0)
        def _():
            q, g = q_ref[here, :], g_ref[here, :]
            lse2 = stat_ref[slot, pl.ds(head, 1), :] * LOG2E
            delta = stat_ref[slot, pl.ds(heads + head, 1), :]
            dq, dk, dv = piece(k_ref[...], k_t, v_ref[...], q, g, lse2, delta, scale)
            acc_k[...] += dk
            acc_v[...] += dv
            dq_ref[here, :] = (dq.T * scale).astype(dq_ref.dtype)

        @pl.when(mark_ref[slot] <= 0)
        def _():
            dq_ref[here, :] = jnp.zeros((QB, q_ref.shape[1]), dq_ref.dtype)

    dk_ref[0] = (acc_k[...] * scale).astype(dk_ref.dtype)
    dv_ref[0] = acc_v[...].astype(dv_ref.dtype)


def merge_kernel(first_ref, second_ref, own_ref, back_ref, out_ref):
    for block in range(own_ref.shape[0] // QB):
        here = pl.ds(block * QB, QB)
        total = own_ref[here, :]
        for pick_ref in (first_ref, second_ref):
            pick = pick_ref[block]
            part = back_ref[jnp.maximum(pick, 0)].astype(jnp.float32)
            total += jnp.where(pick >= 0, part, 0.0)
        out_ref[here, :] = total.astype(out_ref.dtype)


def body(queries, key_rows, value_rows, out_grad, outputs, logsumexp, selections):
    rows, kv, local, hd = queries.shape
    width = kv * local * hd
    heads = kv * local
    blocks = rows // QB
    peers = lax.axis_size("ctx")
    device = lax.axis_index("ctx")
    scale = hd ** (-0.5)
    f32, bf16 = jnp.float32, jnp.bfloat16
    params = pltpu.CompilerParams(vmem_limit_bytes=VMEM_LIMIT)

    q2 = queries.reshape(rows, width)
    g2 = out_grad.reshape(rows, width)
    k2 = key_rows.reshape(rows, kv * hd)
    v2 = value_rows.reshape(rows, kv * hd)
    lse = logsumexp.reshape(heads, rows)
    delta = jnp.transpose(
        jnp.sum((out_grad.astype(f32) * outputs.astype(f32)).reshape(rows, heads, hd), -1)
    )

    peer_ids = jnp.arange(peers, dtype=jnp.int32)
    block_ids = jnp.arange(blocks, dtype=jnp.int32)
    match = jnp.any(selections[:, 1:, None] == peer_ids, axis=1) & (peer_ids != device)
    live = jnp.any(match, axis=0)
    source = jnp.sum(jnp.where(match, block_ids[:, None], 0), axis=0)
    stats = jnp.concatenate([lse, delta], 0).reshape(2 * heads, blocks, QB).transpose(1, 0, 2)
    smem = pl.BlockSpec(memory_space=pltpu.SMEM)
    vmem = pl.BlockSpec(memory_space=pltpu.VMEM)
    q_blocks, g_blocks, send_stat = pl.pallas_call(
        pick_kernel,
        in_specs=[smem, smem, vmem, vmem, vmem],
        out_specs=[vmem] * 3,
        out_shape=[
            jax.ShapeDtypeStruct((peers, QB, width), bf16),
            jax.ShapeDtypeStruct((peers, QB, width), bf16),
            jax.ShapeDtypeStruct((peers, 3 * heads, QB), f32),
        ],
        compiler_params=params,
        name="pick",
    )(
        source,
        live.astype(jnp.int32),
        q2.reshape(blocks, QB, width),
        g2.reshape(blocks, QB, width),
        stats,
    )
    swap = functools.partial(
        lax.all_to_all, axis_name="ctx", split_axis=0, concat_axis=0, tiled=True
    )
    got_stat = swap(send_stat)
    got_q = swap(q_blocks).reshape(peers * QB, width)
    got_g = swap(g_blocks).reshape(peers * QB, width)

    column = lambda n: pl.BlockSpec((n, hd), lambda h, *_: (0, h))
    keys = pl.BlockSpec((rows, hd), lambda h, *_: (0, h // local))
    row = pl.BlockSpec((1, 1, rows), lambda h, *_: (h, 0, 0))
    own_q, own_k, own_v = pl.pallas_call(
        functools.partial(own_kernel, scale),
        grid=(heads,),
        in_specs=[column(rows), column(rows), keys, keys, row, row],
        out_specs=[column(rows)] * 3,
        out_shape=[jax.ShapeDtypeStruct((rows, width), f32)] * 3,
        compiler_params=params,
        name="own",
    )(q2, g2, k2, v2, lse.reshape(heads, 1, rows), delta.reshape(heads, 1, rows))

    marks = (got_stat[:, 2 * heads, 0] > 0).astype(jnp.int32)
    stacked = pl.BlockSpec((1, rows, hd), lambda h, *_: (h, 0, 0))
    dq_out, dk, dv = pl.pallas_call(
        functools.partial(slots_kernel, scale),
        grid_spec=pltpu.PrefetchScalarGridSpec(
            num_scalar_prefetch=1,
            grid=(heads,),
            in_specs=[
                column(peers * QB),
                column(peers * QB),
                pl.BlockSpec(got_stat.shape, lambda h, *_: (0, 0, 0)),
                keys,
                keys,
                column(rows),
                column(rows),
            ],
            out_specs=[column(peers * QB), stacked, stacked],
            scratch_shapes=[pltpu.VMEM((rows, hd), f32)] * 2,
        ),
        out_shape=[
            jax.ShapeDtypeStruct((peers * QB, width), bf16),
            jax.ShapeDtypeStruct((heads, rows, hd), bf16),
            jax.ShapeDtypeStruct((heads, rows, hd), bf16),
        ],
        compiler_params=params,
        name="slots",
    )(marks, got_q, got_g, got_stat, k2, v2, own_k, own_v)

    back = swap(dq_out.reshape(peers, QB, width))
    to_head = functools.partial(
        lax.all_to_all, axis_name="head", split_axis=0, concat_axis=0, tiled=True
    )
    shards = lax.axis_size("head")

    def reduce_heads(part):
        part = to_head(part).reshape(shards, kv // shards, local, rows, hd)
        total = jnp.sum(part.astype(f32), axis=(0, 2))
        return jnp.transpose(total, (1, 0, 2)).astype(bf16)

    first, second = selections[:, 1], selections[:, 2]
    first = jnp.where(first != device, first, -1)
    second = jnp.where((second != device) & (second != first), second, -1)
    grad_q = pl.pallas_call(
        merge_kernel,
        in_specs=[smem, smem, vmem, vmem],
        out_specs=vmem,
        out_shape=jax.ShapeDtypeStruct((rows, width), bf16),
        compiler_params=params,
        name="merge",
    )(first, second, own_q, back)
    return (grad_q.reshape(rows, kv, local, hd), reduce_heads(dk), reduce_heads(dv))


def solution(mesh):
    in_specs = (
        P("ctx", None, "head", None),
        P("ctx", None, None),
        P("ctx", None, None),
        P("ctx", None, "head", None),
        P("ctx", None, "head", None),
        P(None, "head", "ctx"),
        P("ctx", None),
    )
    out_specs = (P("ctx", None, "head", None), P("ctx", "head", None), P("ctx", "head", None))
    return jax.shard_map(body, mesh=mesh, in_specs=in_specs, out_specs=out_specs, check_vma=False)
```

time: 225 us -> 168 us (0.75)
  blocking collectives: 0 us -> 75.1 us
  matrix products: 73.5 us -> 0 us
  Pallas kernels: 0 us -> 35.8 us
  local copies, waits for them, and re-layouts: 33.4 us -> 9.61 us
  starting transfers between devices: 29.9 us -> 7.8 us
  other arithmetic: 25.7 us -> 4.63 us
  between operations: 14.3 us -> 0.82 us
  waiting for transfers between devices: 44.5 us -> 31.2 us
    all_to_all x0 -> x4, blocking collectives: none -> 75.1 us  [the longest x2 36 us: reduce_heads(): part = to_head(part).reshape(shards, kv // shards, local, rows, hd)]
    dot_general x16 -> x0, matrix products: 73.5 us -> none  [the longest x3 16.7 us: slot_grads(): jnp.einsum('srkgd,ckd->skgrc', grad_part, value_part, preferred_element_t...]
    pallas_call x0 -> x4, Pallas kernels: none -> 35.8 us  [the longest x1 21 us: body(): pl.pallas_call(functools.partial(slots_kernel, scale), grid_spec=pltpu.Pr...]
    all_to_all x6 -> x2, starting transfers between devices: 29.6 us -> 7.8 us  [the longest x1 4.24 us: body(): got_g = swap(g_blocks).reshape(peers * QB, width)]
    add x5 -> x0, other arithmetic: 12.6 us -> none  [the longest x4 12.6 us: group_step(): return (dq_slots, acc_k + group_k, acc_v + group_v)]
    gather x10 -> x0, local copies, waits for them, and re-layouts: 11.9 us -> none  [the longest x1 2.27 us: body(): jnp.take(dq_sorted, restore, axis=0).reshape(peers, QB, kv_heads, width)]
    all_to_all x6 -> x2, waiting for transfers between devices: 41.1 us -> 31.2 us  [the longest x1 22.6 us: body(): back = swap(dq_out.reshape(peers, QB, width))]
    unnamed x26 -> x16, local copies, waits for them, and re-layouts: 6.27 us -> 2.57 us
  transfers between devices with their start and end apart: 8 -> 2, of which waited for: 4 -> 2; matrix products, arithmetic and copies ran while one was open for 38% -> 2% of each run, Pallas kernels for 0% -> 7%
where the time goes in v1:
time: 168 us; the launch traced here: 165 us
  blocking collectives  75.1 us (45%)
  Pallas kernels  35.8 us (21%)
  waiting for transfers between devices  31.2 us (19%)
  local copies, waits for them, and re-layouts  9.61 us (6%)
  starting transfers between devices  7.8 us (5%)
  other arithmetic  4.63 us (3%)
    all_to_all x2, blocking collectives, reduce_heads(): part = to_head(part).reshape(shards, kv // shards, local, rows, hd)  36 us
    all_to_all x1, blocking collectives, body(): got_q = swap(q_blocks).reshape(peers * QB, width)  27.2 us
    all_to_all x1, waiting for transfers between devices, body(): back = swap(dq_out.reshape(peers, QB, width))  22.6 us
    pallas_call x1, Pallas kernels, body(): pl.pallas_call(functools.partial(slots_kernel, scale), grid_spec=pltpu.Pr...  21 us
    pallas_call x1, Pallas kernels, body(): pl.pallas_call(functools.partial(own_kernel, scale), grid=(heads,), in_sp...  12.1 us
    all_to_all x1, blocking collectives, body(): got_stat = swap(send_stat)  11.9 us
    all_to_all x1, waiting for transfers between devices, body(): got_g = swap(g_blocks).reshape(peers * QB, width)  8.57 us
    all_to_all x1, starting transfers between devices, body(): got_g = swap(g_blocks).reshape(peers * QB, width)  4.24 us
  transfers between devices with their start and end apart: 2, of which 2 were waited for; matrix products, arithmetic and copies ran while one was open for 2% of the time, Pallas kernels for 7%

profile of v1, /device:TPU:1, one launch (start us, length us, event | category | flops | bytes accessed | tf_op | source)
XLA Modules:
  0.0 164.9 jit_solution(14164808920671836310)
XLA Ops:
  0.6 0.0 copy-start.4
  0.7 0.8 slice.14
  1.4 0.1 fusion
  1.6 1.5 reshape_reshape.7.g_ref
  3.0 0.0 copy-done.4
  3.0 0.0 copy-start.3
  3.1 2.4 %multiply_reduce_fusion = f32[1024,4]{1,0:T(8,128)S(1)} fusion(bf16[1024,4,1,128]{3,1,2,0:T(4,128)(2,1)} %param.11, bf16[1024,4,1,128]{3,1,2,0:T(4,128)(2,1)S(1)} %copy-done.4), kind=kLoop, calls=%fused_computation | loop fusion | flops 2093056 | bytes 2113536 | tf_op jit(solution)/shard_map/reduce_sum | solution.py:125
  5.5 0.2 copy.19
  5.7 1.5 reshape_reshape.6.q_ref
  7.2 1.7 %pick.1 = (bf16[8,128,512]{2,1,0:T(8,128)(2,1)S(1)}, bf16[8,128,512]{2,1,0:T(8,128)(2,1)}, f32[8,12,128]{2,1,0:T(8,128)S(1)}) custom-call(s32[8]{0:T(128)S(1)} %select_reduce_fusion.source_ref, s32[8]{0:T(128)S(1)} %convert_element_type.44.live_ref, bf16[8,128,512]{2,1,0:T(8,128)(2,1)S(1)} %reshape_reshape.6.q_ref, ...), custom_call_target="tpu_custom_call" | custom-call | tf_op jit(solution)/shard_map/pick/pallas_call | solution.py:136
  8.9 11.9 %all_to_all.30.stat_ref = f32[8,12,128]{2,1,0:T(8,128)S(1)} all-to-all(f32[8,12,128]{2,1,0:T(8,128)S(1)} %get-tuple-element.13), channel_id=1, replica_groups=mesh['ctx'=8,'head'=4] {'ctx'}, dimensions={0} | all-to-all | bytes 98304 | tf_op jit(solution)/shard_map/all_to_all | solution.py:157
  20.8 27.2 %all_to_all.31 = bf16[8,128,512]{2,1,0:T(8,128)(2,1)S(1)} all-to-all(bf16[8,128,512]{2,1,0:T(8,128)(2,1)S(1)} %get-tuple-element.14), channel_id=1, replica_groups=mesh['ctx'=8,'head'=4] {'ctx'}, dimensions={0} | all-to-all | bytes 2097152 | tf_op jit(solution)/shard_map/all_to_all | solution.py:158
  48.0 4.2 %all-to-all-start.2 = ((bf16[8,128,512]{2,1,0:T(8,128)(2,1)}), bf16[8,128,512]{2,1,0:T(8,128)(2,1)}, u32[]{:S(2)}, u32[]{:S(2)}) async-start(bf16[8,128,512]{2,1,0:T(8,128)(2,1)} %get-tuple-element.15), calls=%async_computation.2 | async-start | bytes 2097152 | tf_op jit(solution)/shard_map/all_to_all | solution.py:159
  52.3 0.0 copy-done.6
  52.3 0.0 copy-start.5
  52.3 1.7 %copy_bitcast_fusion = (bf16[1024,512]{1,0:T(8,128)(2,1)S(1)}, bf16[1024,512]{1,0:T(8,128)(2,1)S(1)}) fusion(bf16[128,8,4,128]{3,2,1,0:T(4,128)(2,1)S(1)} %bitcast.43, bf16[128,8,4,128]{3,2,1,0:T(4,128)(2,1)} %bitcast.44), kind=kLoop, calls=%fused_computation.1 | loop fusion | bytes 4194304 | tf_op jit(solution)/shard_map/reshape | solution.py:122
  54.0 0.4 copy_bitcast_fusion.2
  54.3 0.7 copy-done
  55.0 0.3 copy-done.1
  55.3 12.1 %own.1 = (f32[1024,512]{1,0:T(8,128)}, f32[1024,512]{1,0:T(8,128)}, f32[1024,512]{1,0:T(8,128)}) custom-call(bf16[1024,512]{1,0:T(8,128)(2,1)S(1)} %get-tuple-element.38.q_ref, bf16[1024,512]{1,0:T(8,128)(2,1)S(1)} %get-tuple-element.37.g_ref, bf16[1024,512]{1,0:T(8,128)(2,1)S(1)} %get-tuple-element.36.k_ref, bf16[1024,512]{1,0:T(8,128)(2,1)S(1)} %get-tuple-element.35.v_ref, ...), custom_call_target="tpu_custom_call" | custom-call | tf_op jit(solution)/shard_map/own/pallas_call | solution.py:164
  67.4 0.2 fusion.1.mark_ref
  67.7 8.6 %all-to-all-done.2 = bf16[8,128,512]{2,1,0:T(8,128)(2,1)} async-done(((bf16[8,128,512]{2,1,0:T(8,128)(2,1)}), bf16[8,128,512]{2,1,0:T(8,128)(2,1)}, u32[]{:S(2)}, u32[]{:S(2)}) %all-to-all-start.2) | async-done | bytes 1048608 | tf_op jit(solution)/shard_map/all_to_all | solution.py:159
  76.2 21.0 %slots.1 = (bf16[1024,512]{1,0:T(8,128)(2,1)}, bf16[4,1024,128]{2,1,0:T(8,128)(2,1)S(1)}, bf16[4,1024,128]{2,1,0:T(8,128)(2,1)S(1)}) custom-call(s32[8]{0:T(128)S(1)} %fusion.1.mark_ref, bf16[1024,512]{1,0:T(8,128)(2,1)S(1)} %bitcast.38, bf16[1024,512]{1,0:T(8,128)(2,1)} %bitcast.7.g_ref, f32[8,12,128]{2,1,0:T(8,128)S(1)} %all_to_all.30.stat_ref, ...), custom_call_target="tpu_custom_call" | custom-call | tf_op jit(solution)/shard_map/slots/pallas_call | solution.py:176
  97.2 19.0 %all_to_all.32 = bf16[4,1024,128]{2,1,0:T(8,128)(2,1)S(1)} all-to-all(bf16[4,1024,128]{2,1,0:T(8,128)(2,1)S(1)} %get-tuple-element.19), channel_id=1, replica_groups=mesh['ctx'=8,'head'=4] {'head'}, dimensions={0} | all-to-all | bytes 2097152 | tf_op jit(solution)/shard_map/all_to_all | solution.py:209
  116.2 17.0 %all_to_all.33 = bf16[4,1024,128]{2,1,0:T(8,128)(2,1)S(1)} all-to-all(bf16[4,1024,128]{2,1,0:T(8,128)(2,1)S(1)} %get-tuple-element.20), channel_id=1, replica_groups=mesh['ctx'=8,'head'=4] {'head'}, dimensions={0} | all-to-all | bytes 2097152 | tf_op jit(solution)/shard_map/all_to_all | solution.py:209
  133.2 3.6 %all-to-all-start.3 = ((bf16[8,128,512]{2,1,0:T(8,128)(2,1)}), bf16[8,128,512]{2,1,0:T(8,128)(2,1)S(1)}, u32[]{:S(2)}, u32[]{:S(2)}) async-start(bf16[8,128,512]{2,1,0:T(8,128)(2,1)} %bitcast.8), calls=%async_computation.3 | async-start | bytes 2097152 | tf_op jit(solution)/shard_map/all_to_all | solution.py:202
  136.8 0.9 reduce_sum.44
  137.7 0.9 reduce_sum.45
  138.6 22.6 %all-to-all-done.3.back_ref = bf16[8,128,512]{2,1,0:T(8,128)(2,1)S(1)} async-done(((bf16[8,128,512]{2,1,0:T(8,128)(2,1)}), bf16[8,128,512]{2,1,0:T(8,128)(2,1)S(1)}, u32[]{:S(2)}, u32[]{:S(2)}) %all-to-all-start.3) | async-done | bytes 1048608 | tf_op jit(solution)/shard_map/all_to_all | solution.py:202
  161.2 1.6 copy-done.2
  162.8 1.0 merge.1
  163.8 1.1 reshape.84
  (16 shorter events, 0.1 us)
Async XLA Ops:
  0.6 2.4 %copy-start.4 = (bf16[1024,4,1,128]{3,1,2,0:T(4,128)(2,1)S(1)}, bf16[1024,4,1,128]{3,1,2,0:T(4,128)(2,1)}, u32[]{:S(2)}) copy-start(bf16[1024,4,1,128]{3,1,2,0:T(4,128)(2,1)} %param.10) | copy-start | bytes 3145732
  3.0 2.6 %copy-start.3 = (f32[4,1,1024]{2,1,0:T(1,128)S(1)}, f32[4,1,1024]{2,1,0:T(1,128)}, u32[]{:S(2)}) copy-start(f32[4,1,1024]{2,1,0:T(1,128)} %lse_ref.1) | copy-start | bytes 49156
  20.8 31.5 %copy-start.6 = (bf16[1024,4,128]{2,1,0:T(4,128)(2,1)S(1)}, bf16[1024,4,128]{2,1,0:T(4,128)(2,1)}, u32[]{:S(2)}) copy-start(bf16[1024,4,128]{2,1,0:T(4,128)(2,1)} %param.9) | copy-start | bytes 3145732
  48.0 28.2 %all-to-all-start.2 = ((bf16[8,128,512]{2,1,0:T(8,128)(2,1)}), bf16[8,128,512]{2,1,0:T(8,128)(2,1)}, u32[]{:S(2)}, u32[]{:S(2)}) async-start(bf16[8,128,512]{2,1,0:T(8,128)(2,1)} %get-tuple-element.15), calls=%async_computation.2 | async-start | bytes 2097152 | tf_op jit(solution)/shard_map/all_to_all | solution.py:159
  52.3 1.7 %copy-start.5 = (bf16[1024,4,1,128]{3,1,2,0:T(4,128)(2,1)S(1)}, bf16[1024,4,1,128]{3,1,2,0:T(4,128)(2,1)}, u32[]{:S(2)}) copy-start(bf16[1024,4,1,128]{3,1,2,0:T(4,128)(2,1)} %param.7) | copy-start | bytes 3145732
  53.9 1.1 copy-start
  54.0 1.3 copy-start.1
  116.2 20.6 %copy-start.7 = (s32[8,3]{0,1:T(4,128)S(1)}, s32[8,3]{0,1:T(4,128)}, u32[]{:S(2)}) copy-start(s32[8,3]{0,1:T(4,128)} %param.13) | copy-start | bytes 292
  133.2 28.0 %all-to-all-start.3 = ((bf16[8,128,512]{2,1,0:T(8,128)(2,1)}), bf16[8,128,512]{2,1,0:T(8,128)(2,1)S(1)}, u32[]{:S(2)}, u32[]{:S(2)}) async-start(bf16[8,128,512]{2,1,0:T(8,128)(2,1)} %bitcast.8), calls=%async_computation.3 | async-start | bytes 2097152 | tf_op jit(solution)/shard_map/all_to_all | solution.py:202
  161.2 1.6 copy-start.2

commit v2 on v1

--- a/solution.py
+++ b/solution.py
@@ -103,6 +103,104 @@
             part = back_ref[jnp.maximum(pick, 0)].astype(jnp.float32)
             total += jnp.where(pick >= 0, part, 0.0)
         out_ref[here, :] = total.astype(out_ref.dtype)
+
+
+def start_ctx(plan, me, peers, way, refs, outs, send_sem, recv_sem):
+    for start in (True, False):
+        for step in range(1, peers):
+            target, origin = me + way * step, me - way * step
+
+            @pl.when((target >= 0) & (target < peers))
+            def _():
+                for i, (ref, out) in enumerate(zip(refs, outs)):
+                    copy = pltpu.make_async_remote_copy(
+                        src_ref=ref.at[target],
+                        dst_ref=out.at[me],
+                        send_sem=send_sem.at[i, target],
+                        recv_sem=recv_sem.at[i, me],
+                        device_id={"ctx": target},
+                        device_id_type=pl.DeviceIdType.MESH,
+                    )
+                    if start and plan != "wait":
+                        copy.start()
+                    if not start and plan != "start":
+                        copy.wait_send()
+
+            if not start and plan != "start":
+
+                @pl.when((origin >= 0) & (origin < peers))
+                def _():
+                    for i, (ref, out) in enumerate(zip(refs, outs)):
+                        pltpu.make_async_remote_copy(
+                            src_ref=ref.at[origin],
+                            dst_ref=out.at[origin],
+                            send_sem=send_sem.at[i, origin],
+                            recv_sem=recv_sem.at[i, origin],
+                            device_id={"ctx": origin},
+                            device_id_type=pl.DeviceIdType.MESH,
+                        ).wait_recv()
+
+
+def greet(axis, me, count, barrier):
+    for step in range(1, count):
+        pl.semaphore_signal(
+            barrier,
+            inc=1,
+            device_id={axis: lax.rem(me + step, count)},
+            device_id_type=pl.DeviceIdType.MESH,
+        )
+
+
+def send_kernel(peers, q_ref, g_ref, stat_ref, q_out, g_out, stat_out, send_sem, recv_sem):
+    me = lax.axis_index("ctx")
+    barrier = pltpu.get_barrier_semaphore()
+    greet("ctx", me, peers, barrier)
+    pl.semaphore_wait(barrier, peers - 1)
+    start_ctx(
+        "both", me, peers, -1, (stat_ref, q_ref, g_ref), (stat_out, q_out, g_out), send_sem, recv_sem
+    )
+
+
+def return_kernel(
+    peers, shards, dq_ref, dk_ref, dv_ref, dq_out, dk_out, dv_out,
+    send_sem, recv_sem, head_send, head_recv, local_sem,
+):
+    me, mine = lax.axis_index("ctx"), lax.axis_index("head")
+    barrier = pltpu.get_barrier_semaphore()
+    greet("ctx", me, peers, barrier)
+    greet("head", mine, shards, barrier)
+    pl.semaphore_wait(barrier, peers - 1 + shards - 1)
+    pairs = ((dk_ref, dk_out), (dv_ref, dv_out))
+
+    def head_copy(i, step):
+        target = lax.rem(mine + step, shards)
+        return pltpu.make_async_remote_copy(
+            src_ref=pairs[i][0].at[target],
+            dst_ref=pairs[i][1].at[mine],
+            send_sem=head_send.at[i, step],
+            recv_sem=head_recv.at[i, step],
+            device_id={"head": target},
+            device_id_type=pl.DeviceIdType.MESH,
+        )
+
+    start_ctx("start", me, peers, 1, (dq_ref,), (dq_out,), send_sem, recv_sem)
+    for step in range(1, shards):
+        for i in range(2):
+            head_copy(i, step).start()
+    keeps = [
+        pltpu.make_async_copy(ref.at[mine], out.at[mine], local_sem.at[i])
+        for i, (ref, out) in enumerate(pairs)
+    ]
+    for keep in keeps:
+        keep.start()
+    for keep in keeps:
+        keep.wait()
+    for step in range(1, shards):
+        for i in range(2):
+            copy = head_copy(i, step)
+            copy.wait_send()
+            copy.wait_recv()
+    start_ctx("wait", me, peers, 1, (dq_ref,), (dq_out,), send_sem, recv_sem)
 
 
 def body(queries, key_rows, value_rows, out_grad, outputs, logsumexp, selections):
@@ -151,12 +249,20 @@
         g2.reshape(blocks, QB, width),
         stats,
     )
-    swap = functools.partial(
-        lax.all_to_all, axis_name="ctx", split_axis=0, concat_axis=0, tiled=True
-    )
-    got_stat = swap(send_stat)
-    got_q = swap(q_blocks).reshape(peers * QB, width)
-    got_g = swap(g_blocks).reshape(peers * QB, width)
+    anywhere = pl.BlockSpec(memory_space=pl.ANY)
+    dma = lambda *shape: pltpu.SemaphoreType.DMA(shape)
+    like = lambda *arrays: [jax.ShapeDtypeStruct(x.shape, x.dtype) for x in arrays]
+    got_q, got_g, got_stat = pl.pallas_call(
+        functools.partial(send_kernel, peers),
+        in_specs=[anywhere] * 3,
+        out_specs=[anywhere] * 3,
+        out_shape=like(q_blocks, g_blocks, send_stat),
+        scratch_shapes=[dma(3, peers), dma(3, peers)],
+        compiler_params=pltpu.CompilerParams(collective_id=0, has_side_effects=True),
+        name="send",
+    )(q_blocks, g_blocks, send_stat)
+    got_q = got_q.reshape(peers * QB, width)
+    got_g = got_g.reshape(peers * QB, width)
 
     column = lambda n: pl.BlockSpec((n, hd), lambda h, *_: (0, h))
     keys = pl.BlockSpec((rows, hd), lambda h, *_: (0, h // local))
@@ -171,7 +277,7 @@
         name="own",
     )(q2, g2, k2, v2, lse.reshape(heads, 1, rows), delta.reshape(heads, 1, rows))
 
-    marks = (got_stat[:, 2 * heads, 0] > 0).astype(jnp.int32)
+    marks = ((got_stat[:, 2 * heads, 0] > 0) & (peer_ids > device)).astype(jnp.int32)
     stacked = pl.BlockSpec((1, rows, hd), lambda h, *_: (h, 0, 0))
     dq_out, dk, dv = pl.pallas_call(
         functools.partial(slots_kernel, scale),
@@ -199,14 +305,24 @@
         name="slots",
     )(marks, got_q, got_g, got_stat, k2, v2, own_k, own_v)
 
-    back = swap(dq_out.reshape(peers, QB, width))
-    to_head = functools.partial(
-        lax.all_to_all, axis_name="head", split_axis=0, concat_axis=0, tiled=True
-    )
     shards = lax.axis_size("head")
+    dq_out = dq_out.reshape(peers, QB, width)
+    dk = dk.reshape(shards, heads // shards, rows, hd)
+    dv = dv.reshape(shards, heads // shards, rows, hd)
+    back, dk, dv = pl.pallas_call(
+        functools.partial(return_kernel, peers, shards),
+        in_specs=[anywhere] * 3,
+        out_specs=[anywhere] * 3,
+        out_shape=like(dq_out, dk, dv),
+        scratch_shapes=[
+            dma(1, peers), dma(1, peers), dma(2, shards), dma(2, shards), dma(2),
+        ],
+        compiler_params=pltpu.CompilerParams(collective_id=1, has_side_effects=True),
+        name="give_back",
+    )(dq_out, dk, dv)
 
     def reduce_heads(part):
-        part = to_head(part).reshape(shards, kv // shards, local, rows, hd)
+        part = part.reshape(shards, kv // shards, local, rows, hd)
         total = jnp.sum(part.astype(f32), axis=(0, 2))
         return jnp.transpose(total, (1, 0, 2)).astype(bf16)
 

time: 168 us -> 133 us (0.79); the launches traced: 165 us -> 132 us
  Pallas kernels: 35.8 us -> 114 us
  blocking collectives: 75.1 us -> 0 us
  waiting for transfers between devices: 31.2 us -> 0 us
  starting transfers between devices: 7.8 us -> 0 us
  local copies, waits for them, and re-layouts: 9.61 us -> 11.8 us
    pallas_call x0 -> x2, Pallas kernels: none -> 79.2 us  [the longest x1 52.2 us: body(): pl.pallas_call(functools.partial(send_kernel, peers), in_specs=[anywhere]...]
    all_to_all x4 -> x0, blocking collectives: 75.1 us -> none  [the longest x2 36 us: reduce_heads(): part = to_head(part).reshape(shards, kv // shards, local, rows, hd)]
    all_to_all x2 -> x0, waiting for transfers between devices: 31.2 us -> none  [the longest x1 22.6 us: body(): back = swap(dq_out.reshape(peers, QB, width))]
    all_to_all x2 -> x0, starting transfers between devices: 7.8 us -> none  [the longest x1 4.24 us: body(): got_g = swap(g_blocks).reshape(peers * QB, width)]
    unnamed x16 -> x44, local copies, waits for them, and re-layouts: 2.57 us -> 8.06 us
  transfers between devices with their start and end apart: 2 -> 0, of which waited for: 2 -> 0; matrix products, arithmetic and copies ran while one was open for 2% -> 0% of each run, Pallas kernels for 7% -> 0%
where the time goes in v2:
time: 133 us; the launch traced here: 132 us
  Pallas kernels  114 us (86%)
  local copies, waits for them, and re-layouts  11.8 us (9%)
  other arithmetic  5.79 us (4%)
    pallas_call x1, Pallas kernels, body(): pl.pallas_call(functools.partial(send_kernel, peers), in_specs=[anywhere]...  52.2 us
    pallas_call x1, Pallas kernels, body(): pl.pallas_call(functools.partial(return_kernel, peers, shards), in_specs=...  27 us
    pallas_call x1, Pallas kernels, body(): pl.pallas_call(functools.partial(slots_kernel, scale), grid_spec=pltpu.Pr...  20.5 us
    pallas_call x1, Pallas kernels, body(): pl.pallas_call(functools.partial(own_kernel, scale), grid=(heads,), in_sp...  12.2 us
    unnamed x44, local copies, waits for them, and re-layouts  8.06 us
    reduce_sum x1, other arithmetic, body(): jnp.sum((out_grad.astype(f32) * outputs.astype(f32)).reshape(rows, heads,...  2.83 us

profile of v2, /device:TPU:1, one launch (start us, length us, event | category | flops | bytes accessed | tf_op | source)
XLA Modules:
  0.0 132.2 jit_solution(5439310852721392907)
XLA Ops:
  0.6 0.0 copy-start.15
  0.7 0.8 slice.14
  1.4 0.1 fusion
  1.6 2.8 %multiply_reduce_fusion = f32[1024,4]{1,0:T(8,128)S(1)} fusion(bf16[1024,4,1,128]{3,1,2,0:T(4,128)(2,1)} %param.11, bf16[1024,4,1,128]{3,1,2,0:T(4,128)(2,1)} %param.10), kind=kLoop, calls=%fused_computation | loop fusion | flops 2093056 | bytes 2113536 | tf_op jit(solution)/shard_map/reduce_sum | solution.py:223
  4.4 0.2 copy.19
  4.6 0.4 reshape_reshape.6.q_ref
  5.1 0.4 reshape_reshape.7.g_ref
  5.6 0.7 pick.1
  6.2 0.0 copy-start.9
  6.3 1.0 copy-done.9
  7.2 1.0 copy-done.10
  8.2 0.6 copy-done.13
  8.8 52.2 %send.1 = (bf16[8,128,512]{2,1,0:T(8,128)(2,1)}, bf16[8,128,512]{2,1,0:T(8,128)(2,1)}, f32[8,12,128]{2,1,0:T(8,128)}) custom-call(bf16[8,128,512]{2,1,0:T(8,128)(2,1)} %copy-done.9, bf16[8,128,512]{2,1,0:T(8,128)(2,1)} %copy-done.10, f32[8,12,128]{2,1,0:T(8,128)} %copy-done.13), custom_call_target="tpu_custom_call" | custom-call | tf_op jit(solution)/shard_map/send/pallas_call | solution.py:255
  61.0 1.0 compare_reduce_fusion
  62.1 0.0 copy-start.16
  62.1 0.3 copy_bitcast_fusion
  62.4 0.0 copy-start.1
  62.4 0.8 copy-done.16
  63.3 0.4 copy_bitcast_fusion.2
  63.8 12.2 %own.1 = (f32[1024,512]{1,0:T(8,128)}, f32[1024,512]{1,0:T(8,128)}, f32[1024,512]{1,0:T(8,128)}) custom-call(bf16[1024,512]{1,0:T(8,128)(2,1)S(1)} %get-tuple-element.50.q_ref, bf16[1024,512]{1,0:T(8,128)(2,1)S(1)} %get-tuple-element.49.g_ref, bf16[1024,512]{1,0:T(8,128)(2,1)S(1)} %get-tuple-element.48.k_ref, bf16[1024,512]{1,0:T(8,128)(2,1)S(1)} %get-tuple-element.47.v_ref, ...), custom_call_target="tpu_custom_call" | custom-call | tf_op jit(solution)/shard_map/own/pallas_call | solution.py:270
  76.0 20.5 %slots.1 = (bf16[1024,512]{1,0:T(8,128)(2,1)S(1)}, bf16[4,1024,128]{2,1,0:T(8,128)(2,1)S(1)}, bf16[4,1024,128]{2,1,0:T(8,128)(2,1)S(1)}) custom-call(s32[8]{0:T(128)S(1)} %and_convert_fusion.mark_ref, bf16[1024,512]{1,0:T(8,128)(2,1)S(1)} %bitcast.40, bf16[1024,512]{1,0:T(8,128)(2,1)S(1)} %bitcast.41, f32[8,12,128]{2,1,0:T(8,128)S(1)} %copy-done.11, ...), custom_call_target="tpu_custom_call" | custom-call | tf_op jit(solution)/shard_map/slots/pallas_call | solution.py:282
  96.5 0.0 copy-start.5
  96.6 1.0 copy-done.5
  97.5 1.0 copy-done.6
  98.5 1.0 copy-done.7
  99.5 27.0 %give_back.1 = (bf16[8,128,512]{2,1,0:T(8,128)(2,1)}, bf16[4,1,1024,128]{3,2,1,0:T(8,128)(2,1)}, bf16[4,1,1024,128]{3,2,1,0:T(8,128)(2,1)}) custom-call(bf16[8,128,512]{2,1,0:T(8,128)(2,1)} %bitcast.42, bf16[4,1,1024,128]{3,2,1,0:T(8,128)(2,1)} %bitcast.43, bf16[4,1,1024,128]{3,2,1,0:T(8,128)(2,1)} %bitcast.44), custom_call_target="tpu_custom_call" | custom-call | tf_op jit(solution)/shard_map/give_back/pallas_call | solution.py:312
  126.6 1.2 copy-done.8
  127.8 1.0 merge.1
  128.8 1.1 reshape.94
  129.9 0.4 copy-done.18
  130.4 0.9 reduce_sum.44
  131.3 0.9 reduce_sum.45
  (39 shorter events, 0.2 us)
Async XLA Ops:
  0.6 4.0 %copy-start.12 = (f32[4,1,1024]{2,1,0:T(1,128)S(1)}, f32[4,1,1024]{2,1,0:T(1,128)}, u32[]{:S(2)}) copy-start(f32[4,1,1024]{2,1,0:T(1,128)} %lse_ref.1) | copy-start | bytes 49156
  0.6 4.0 %copy-start.15 = (bf16[1024,4,1,128]{3,1,2,0:T(4,128)(2,1)S(1)}, bf16[1024,4,1,128]{3,1,2,0:T(4,128)(2,1)}, u32[]{:S(2)}) copy-start(bf16[1024,4,1,128]{3,1,2,0:T(4,128)(2,1)} %param.7) | copy-start | bytes 3145732
  1.6 3.5 %copy-start.14 = (bf16[1024,4,1,128]{3,1,2,0:T(4,128)(2,1)S(1)}, bf16[1024,4,1,128]{3,1,2,0:T(4,128)(2,1)}, u32[]{:S(2)}) copy-start(bf16[1024,4,1,128]{3,1,2,0:T(4,128)(2,1)} %param.10) | copy-start | bytes 3145732
  6.2 1.0 copy-start.9
  7.2 1.0 copy-start.10
  8.2 0.6 copy-start.13
  8.8 53.2 %copy-start.19 = (bf16[1024,4,128]{2,1,0:T(4,128)(2,1)S(1)}, bf16[1024,4,128]{2,1,0:T(4,128)(2,1)}, u32[]{:S(2)}) copy-start(bf16[1024,4,128]{2,1,0:T(4,128)(2,1)} %param.9) | copy-start | bytes 3145732
  8.8 53.2 %copy-start.20 = (bf16[1024,4,128]{2,1,0:T(4,128)(2,1)S(1)}, bf16[1024,4,128]{2,1,0:T(4,128)(2,1)}, u32[]{:S(2)}) copy-start(bf16[1024,4,128]{2,1,0:T(4,128)(2,1)} %param.8) | copy-start | bytes 3145732
  62.1 1.2 copy-start.16
  62.4 1.3 copy-start
  62.4 1.3 copy-start.1
  63.7 12.2 %copy-start.3 = (bf16[8,128,512]{2,1,0:T(8,128)(2,1)S(1)}, bf16[8,128,512]{2,1,0:T(8,128)(2,1)}, u32[]{:S(2)}) copy-start(bf16[8,128,512]{2,1,0:T(8,128)(2,1)} %get-tuple-element.23) | copy-start | bytes 3145732
  63.8 12.2 %copy-start.4 = (bf16[8,128,512]{2,1,0:T(8,128)(2,1)S(1)}, bf16[8,128,512]{2,1,0:T(8,128)(2,1)}, u32[]{:S(2)}) copy-start(bf16[8,128,512]{2,1,0:T(8,128)(2,1)} %get-tuple-element.24) | copy-start | bytes 3145732
  63.8 12.2 %copy-start.11 = (f32[8,12,128]{2,1,0:T(8,128)S(1)}, f32[8,12,128]{2,1,0:T(8,128)}, u32[]{:S(2)}) copy-start(f32[8,12,128]{2,1,0:T(8,128)} %get-tuple-element.22.stat_ref) | copy-start | bytes 147460
  96.5 1.0 copy-start.5
  97.5 1.0 copy-start.6
  98.5 1.0 copy-start.7
  99.5 27.0 %copy-start.21 = (s32[8,3]{0,1:T(4,128)S(1)}, s32[8,3]{0,1:T(4,128)}, u32[]{:S(2)}) copy-start(s32[8,3]{0,1:T(4,128)} %param.13) | copy-start | bytes 292
  99.5 27.0 %copy-start.2 = (f32[1024,512]{1,0:T(8,128)S(1)}, f32[1024,512]{1,0:T(8,128)}, u32[]{:S(2)}) copy-start(f32[1024,512]{1,0:T(8,128)} %get-tuple-element.18.own_ref) | copy-start | bytes 6291460
  126.6 1.2 copy-start.8
  128.8 1.6 %copy-start.18 = (bf16[4,1,1024,128]{3,2,1,0:T(8,128)(2,1)S(1)}, bf16[4,1,1024,128]{3,2,1,0:T(8,128)(2,1)}, u32[]{:S(2)}) copy-start(bf16[4,1,1024,128]{3,2,1,0:T(8,128)(2,1)} %get-tuple-element.31) | copy-start | bytes 3145732
  128.8 2.5 %copy-start.17 = (bf16[4,1,1024,128]{3,2,1,0:T(8,128)(2,1)S(1)}, bf16[4,1,1024,128]{3,2,1,0:T(8,128)(2,1)}, u32[]{:S(2)}) copy-start(bf16[4,1,1024,128]{3,2,1,0:T(8,128)(2,1)} %get-tuple-element.32) | copy-start | bytes 3145732

commit v3 on v2

--- a/solution.py
+++ b/solution.py
@@ -151,14 +151,32 @@
         )
 
 
-def send_kernel(peers, q_ref, g_ref, stat_ref, q_out, g_out, stat_out, send_sem, recv_sem):
+def send_kernel(
+    peers, scale, q_ref, g_ref, stat_ref, q_own, g_own, k_ref, v_ref, lse_ref, delta_ref,
+    q_out, g_out, stat_out, dq_ref, dk_ref, dv_ref, send_sem, recv_sem,
+):
     me = lax.axis_index("ctx")
     barrier = pltpu.get_barrier_semaphore()
     greet("ctx", me, peers, barrier)
     pl.semaphore_wait(barrier, peers - 1)
-    start_ctx(
-        "both", me, peers, -1, (stat_ref, q_ref, g_ref), (stat_out, q_out, g_out), send_sem, recv_sem
-    )
+    sent, outs = (stat_ref, q_ref, g_ref), (stat_out, q_out, g_out)
+    start_ctx("start", me, peers, -1, sent, outs, send_sem, recv_sem)
+    heads = lse_ref.shape[0]
+    hd = q_own.shape[1] // heads
+    local = q_own.shape[1] // k_ref.shape[1]
+
+    def one_head(head, carry):
+        at = (slice(None), pl.ds(pl.multiple_of(head * hd, hd), hd))
+        key_at = (slice(None), pl.ds(pl.multiple_of(head // local * hd, hd), hd))
+        row = pl.ds(head, 1)
+        own_kernel(
+            scale, q_own.at[at], g_own.at[at], k_ref.at[key_at], v_ref.at[key_at],
+            lse_ref.at[row], delta_ref.at[row], dq_ref.at[at], dk_ref.at[at], dv_ref.at[at],
+        )
+        return carry
+
+    lax.fori_loop(0, heads, one_head, 0)
+    start_ctx("wait", me, peers, -1, sent, outs, send_sem, recv_sem)
 
 
 def return_kernel(
@@ -252,30 +270,26 @@
     anywhere = pl.BlockSpec(memory_space=pl.ANY)
     dma = lambda *shape: pltpu.SemaphoreType.DMA(shape)
     like = lambda *arrays: [jax.ShapeDtypeStruct(x.shape, x.dtype) for x in arrays]
-    got_q, got_g, got_stat = pl.pallas_call(
-        functools.partial(send_kernel, peers),
-        in_specs=[anywhere] * 3,
-        out_specs=[anywhere] * 3,
-        out_shape=like(q_blocks, g_blocks, send_stat),
+    own_shape = [jax.ShapeDtypeStruct((rows, width), f32)] * 3
+    got_q, got_g, got_stat, own_q, own_k, own_v = pl.pallas_call(
+        functools.partial(send_kernel, peers, scale),
+        in_specs=[anywhere] * 3 + [vmem] * 6,
+        out_specs=[anywhere] * 3 + [vmem] * 3,
+        out_shape=like(q_blocks, g_blocks, send_stat) + own_shape,
         scratch_shapes=[dma(3, peers), dma(3, peers)],
-        compiler_params=pltpu.CompilerParams(collective_id=0, has_side_effects=True),
+        compiler_params=pltpu.CompilerParams(
+            collective_id=0, has_side_effects=True, vmem_limit_bytes=VMEM_LIMIT
+        ),
         name="send",
-    )(q_blocks, g_blocks, send_stat)
+    )(
+        q_blocks, g_blocks, send_stat, q2, g2, k2, v2,
+        lse.reshape(heads, 1, rows), delta.reshape(heads, 1, rows),
+    )
     got_q = got_q.reshape(peers * QB, width)
     got_g = got_g.reshape(peers * QB, width)
 
     column = lambda n: pl.BlockSpec((n, hd), lambda h, *_: (0, h))
     keys = pl.BlockSpec((rows, hd), lambda h, *_: (0, h // local))
-    row = pl.BlockSpec((1, 1, rows), lambda h, *_: (h, 0, 0))
-    own_q, own_k, own_v = pl.pallas_call(
-        functools.partial(own_kernel, scale),
-        grid=(heads,),
-        in_specs=[column(rows), column(rows), keys, keys, row, row],
-        out_specs=[column(rows)] * 3,
-        out_shape=[jax.ShapeDtypeStruct((rows, width), f32)] * 3,
-        compiler_params=params,
-        name="own",
-    )(q2, g2, k2, v2, lse.reshape(heads, 1, rows), delta.reshape(heads, 1, rows))
 
     marks = ((got_stat[:, 2 * heads, 0] > 0) & (peer_ids > device)).astype(jnp.int32)
     stacked = pl.BlockSpec((1, rows, hd), lambda h, *_: (h, 0, 0))

time: 133 us -> 123 us (0.925)
  Pallas kernels: 114 us -> 106 us
    pallas_call x2 -> x1, Pallas kernels: 64.4 us -> 56.4 us  [body(): pl.pallas_call(functools.partial(send_kernel, peers, scale), in_specs=[an...]
    unnamed x44 -> x28, local copies, waits for them, and re-layouts: 8.06 us -> 5.48 us
    reshape x1, local copies, waits for them, and re-layouts: 0.34 us -> 1.68 us  [body(): v2 = value_rows.reshape(rows, kv * hd)]
where the time goes in v3:
time: 123 us
  Pallas kernels  106 us (86%)
  local copies, waits for them, and re-layouts  11.5 us (9%)
  other arithmetic  5.03 us (4%)
    pallas_call x1, Pallas kernels, body(): pl.pallas_call(functools.partial(send_kernel, peers, scale), in_specs=[an...  56.4 us
    pallas_call x1, Pallas kernels, body(): pl.pallas_call(functools.partial(return_kernel, peers, shards), in_specs=...  27 us
    pallas_call x1, Pallas kernels, body(): pl.pallas_call(functools.partial(slots_kernel, scale), grid_spec=pltpu.Pr...  20.5 us
    unnamed x28, local copies, waits for them, and re-layouts  5.48 us
    reduce_sum x1, other arithmetic, body(): jnp.sum((out_grad.astype(f32) * outputs.astype(f32)).reshape(rows, heads,...  2.83 us

profile of v3, /device:TPU:1, one launch (start us, length us, event | category | flops | bytes accessed | tf_op | source)
XLA Modules:
  0.0 122.9 jit_solution(8437153117484184369)
XLA Ops:
  0.6 0.0 copy-start.5
  0.6 0.0 copy-start.7
  0.7 0.8 slice.14
  1.4 0.1 fusion
  1.6 2.8 %multiply_reduce_fusion = f32[1024,4]{1,0:T(8,128)S(1)} fusion(bf16[1024,4,1,128]{3,1,2,0:T(4,128)(2,1)} %param.11, bf16[1024,4,1,128]{3,1,2,0:T(4,128)(2,1)} %param.10), kind=kLoop, calls=%fused_computation | loop fusion | flops 2093056 | bytes 2113536 | tf_op jit(solution)/shard_map/reduce_sum | solution.py:241
  4.4 0.2 copy.22
  4.6 0.0 copy-done.7
  4.6 0.4 reshape_reshape.6.q_ref
  5.1 0.4 reshape_reshape.7.g_ref
  5.6 0.0 copy-start.11
  5.6 0.0 copy-start.12
  5.6 0.7 pick.1
  6.3 0.5 copy-done.11
  6.8 0.3 copy-done.12
  7.1 1.7 %copy_bitcast_fusion = (bf16[1024,512]{1,0:T(8,128)(2,1)}, bf16[1024,512]{1,0:T(8,128)(2,1)}) fusion(bf16[128,8,4,128]{3,2,1,0:T(4,128)(2,1)S(1)} %bitcast.49, bf16[128,8,4,128]{3,2,1,0:T(4,128)(2,1)S(1)} %bitcast.50), kind=kLoop, calls=%fused_computation.1 | loop fusion | bytes 4194304 | tf_op jit(solution)/shard_map/reshape | solution.py:238
  8.8 1.3 %copy_bitcast_fusion.2 = (bf16[1024,512]{1,0:T(8,128)(2,1)}, bf16[1024,512]{1,0:T(8,128)(2,1)S(1)}) fusion(bf16[128,8,4,128]{3,2,1,0:T(4,128)(2,1)S(1)} %bitcast.46, bf16[128,8,4,128]{3,2,1,0:T(4,128)(2,1)S(1)} %bitcast.47), kind=kLoop, calls=%fused_computation.3 | loop fusion | bytes 4194304 | tf_op jit(solution)/shard_map/reshape | solution.py:236
  10.1 56.4 %send.1 = (bf16[8,128,512]{2,1,0:T(8,128)(2,1)S(1)}, bf16[8,128,512]{2,1,0:T(8,128)(2,1)S(1)}, f32[8,12,128]{2,1,0:T(8,128)S(1)}, f32[1024,512]{1,0:T(8,128)}, f32[1024,512]{1,0:T(8,128)}, /*index=5*/f32[1024,512]{1,0:T(8,128)}) custom-call(bf16[8,128,512]{2,1,0:T(8,128)(2,1)S(1)} %get-tuple-element.18.q_ref, ...), custom_call_target="tpu_custom_call" | custom-call | tf_op jit(solution)/shard_map/send/pallas_call | solution.py:274
  66.5 0.2 compare_reduce_fusion
  66.7 20.5 %slots.1 = (bf16[1024,512]{1,0:T(8,128)(2,1)S(1)}, bf16[4,1024,128]{2,1,0:T(8,128)(2,1)S(1)}, bf16[4,1024,128]{2,1,0:T(8,128)(2,1)S(1)}) custom-call(s32[8]{0:T(128)S(1)} %and_convert_fusion.mark_ref, bf16[1024,512]{1,0:T(8,128)(2,1)S(1)} %bitcast.40, bf16[1024,512]{1,0:T(8,128)(2,1)S(1)} %bitcast.41, f32[8,12,128]{2,1,0:T(8,128)S(1)} %get-tuple-element.22.stat_ref, ...), custom_call_target="tpu_custom_call" | custom-call | tf_op jit(solution)/shard_map/slots/pallas_call | solution.py:296
  87.3 0.0 copy-start.1
  87.3 1.0 copy-done.1
  88.2 1.0 copy-done.2
  89.2 1.0 copy-done.3
  90.2 27.0 %give_back.1 = (bf16[8,128,512]{2,1,0:T(8,128)(2,1)}, bf16[4,1,1024,128]{3,2,1,0:T(8,128)(2,1)}, bf16[4,1,1024,128]{3,2,1,0:T(8,128)(2,1)}) custom-call(bf16[8,128,512]{2,1,0:T(8,128)(2,1)} %bitcast.42, bf16[4,1,1024,128]{3,2,1,0:T(8,128)(2,1)} %bitcast.43, bf16[4,1,1024,128]{3,2,1,0:T(8,128)(2,1)} %bitcast.44), custom_call_target="tpu_custom_call" | custom-call | tf_op jit(solution)/shard_map/give_back/pallas_call | solution.py:326
  117.3 0.0 copy-done.13
  117.3 0.0 copy-done
  117.3 1.2 copy-done.4
  118.5 1.0 merge.1
  119.6 1.1 reshape.94
  120.7 0.4 copy-done.10
  121.1 0.9 reduce_sum.44
  122.0 0.9 reduce_sum.45
  (22 shorter events, 0.1 us)
Async XLA Ops:
  0.6 4.0 %copy-start.5 = (f32[4,1,1024]{2,1,0:T(1,128)S(1)}, f32[4,1,1024]{2,1,0:T(1,128)}, u32[]{:S(2)}) copy-start(f32[4,1,1024]{2,1,0:T(1,128)} %lse_ref.1) | copy-start | bytes 49156
  0.6 4.0 %copy-start.7 = (bf16[1024,4,1,128]{3,1,2,0:T(4,128)(2,1)S(1)}, bf16[1024,4,1,128]{3,1,2,0:T(4,128)(2,1)}, u32[]{:S(2)}) copy-start(bf16[1024,4,1,128]{3,1,2,0:T(4,128)(2,1)} %param.7) | copy-start | bytes 3145732
  1.6 3.5 %copy-start.6 = (bf16[1024,4,1,128]{3,1,2,0:T(4,128)(2,1)S(1)}, bf16[1024,4,1,128]{3,1,2,0:T(4,128)(2,1)}, u32[]{:S(2)}) copy-start(bf16[1024,4,1,128]{3,1,2,0:T(4,128)(2,1)} %param.10) | copy-start | bytes 3145732
  5.6 1.2 copy-start.11
  5.6 1.5 %copy-start.12 = (bf16[1024,4,128]{2,1,0:T(4,128)(2,1)S(1)}, bf16[1024,4,128]{2,1,0:T(4,128)(2,1)}, u32[]{:S(2)}) copy-start(bf16[1024,4,128]{2,1,0:T(4,128)(2,1)} %param.8) | copy-start | bytes 3145732
  7.1 1.7 %copy-start.8 = (bf16[1024,4,1,128]{3,1,2,0:T(4,128)(2,1)S(1)}, bf16[1024,4,1,128]{3,1,2,0:T(4,128)(2,1)}, u32[]{:S(2)}) copy-start(bf16[1024,4,1,128]{3,1,2,0:T(4,128)(2,1)} %param.7) | copy-start | bytes 3145732
  87.3 1.0 copy-start.1
  88.2 1.0 copy-start.2
  89.2 1.0 copy-start.3
  90.2 27.0 %copy-start.13 = (s32[8,3]{0,1:T(4,128)S(1)}, s32[8,3]{0,1:T(4,128)}, u32[]{:S(2)}) copy-start(s32[8,3]{0,1:T(4,128)} %param.13) | copy-start | bytes 292
  90.2 27.0 %copy-start = (f32[1024,512]{1,0:T(8,128)S(1)}, f32[1024,512]{1,0:T(8,128)}, u32[]{:S(2)}) copy-start(f32[1024,512]{1,0:T(8,128)} %get-tuple-element.21.own_ref) | copy-start | bytes 6291460
  117.3 1.2 copy-start.4
  119.6 1.6 %copy-start.10 = (bf16[4,1,1024,128]{3,2,1,0:T(8,128)(2,1)S(1)}, bf16[4,1,1024,128]{3,2,1,0:T(8,128)(2,1)}, u32[]{:S(2)}) copy-start(bf16[4,1,1024,128]{3,2,1,0:T(8,128)(2,1)} %get-tuple-element.31) | copy-start | bytes 3145732
  119.6 2.5 %copy-start.9 = (bf16[4,1,1024,128]{3,2,1,0:T(8,128)(2,1)S(1)}, bf16[4,1,1024,128]{3,2,1,0:T(8,128)(2,1)}, u32[]{:S(2)}) copy-start(bf16[4,1,1024,128]{3,2,1,0:T(8,128)(2,1)} %get-tuple-element.32) | copy-start | bytes 3145732

commit v4 on v3

--- a/solution.py
+++ b/solution.py
@@ -62,36 +62,6 @@
             dk_ref[:lo, :] += dk
             dv_ref[:lo, :] += dv
         dq_ref[here, :] = dq.T * scale
-
-
-def slots_kernel(
-    scale, mark_ref, q_ref, g_ref, stat_ref, k_ref, v_ref, dk_in, dv_in, dq_ref, dk_ref, dv_ref,
-    acc_k, acc_v,
-):
-    head = pl.program_id(0)
-    heads = pl.num_programs(0)
-    k_t = k_ref[...].T
-    acc_k[...] = dk_in[...]
-    acc_v[...] = dv_in[...]
-    for slot in range(q_ref.shape[0] // QB):
-        here = pl.ds(slot * QB, QB)
-
-        @pl.when(mark_ref[slot] > 0)
-        def _():
-            q, g = q_ref[here, :], g_ref[here, :]
-            lse2 = stat_ref[slot, pl.ds(head, 1), :] * LOG2E
-            delta = stat_ref[slot, pl.ds(heads + head, 1), :]
-            dq, dk, dv = piece(k_ref[...], k_t, v_ref[...], q, g, lse2, delta, scale)
-            acc_k[...] += dk
-            acc_v[...] += dv
-            dq_ref[here, :] = (dq.T * scale).astype(dq_ref.dtype)
-
-        @pl.when(mark_ref[slot] <= 0)
-        def _():
-            dq_ref[here, :] = jnp.zeros((QB, q_ref.shape[1]), dq_ref.dtype)
-
-    dk_ref[0] = (acc_k[...] * scale).astype(dk_ref.dtype)
-    dv_ref[0] = acc_v[...].astype(dv_ref.dtype)
 
 
 def merge_kernel(first_ref, second_ref, own_ref, back_ref, out_ref):
@@ -121,12 +91,12 @@
                         device_id={"ctx": target},
                         device_id_type=pl.DeviceIdType.MESH,
                     )
-                    if start and plan != "wait":
+                    if start and plan in ("start", "both"):
                         copy.start()
                     if not start and plan != "start":
                         copy.wait_send()
 
-            if not start and plan != "start":
+            if not start and plan in ("wait", "both"):
 
                 @pl.when((origin >= 0) & (origin < peers))
                 def _():
@@ -153,7 +123,8 @@
 
 def send_kernel(
     peers, scale, q_ref, g_ref, stat_ref, q_own, g_own, k_ref, v_ref, lse_ref, delta_ref,
-    q_out, g_out, stat_out, dq_ref, dk_ref, dv_ref, send_sem, recv_sem,
+    q_out, g_out, stat_out, dq_ref, slot_ref, dk_out, dv_out,
+    dk_ref, dv_ref, kt_ref, send_sem, recv_sem,
 ):
     me = lax.axis_index("ctx")
     barrier = pltpu.get_barrier_semaphore()
@@ -176,7 +147,54 @@
         return carry
 
     lax.fori_loop(0, heads, one_head, 0)
-    start_ctx("wait", me, peers, -1, sent, outs, send_sem, recv_sem)
+
+    def turn_keys(head, carry):
+        at = pl.ds(pl.multiple_of(head * hd, hd), hd)
+        kt_ref[at, :] = k_ref[:, at].T
+        return carry
+
+    lax.fori_loop(0, heads // local, turn_keys, 0)
+
+    def one_slot(step, carry):
+        origin = me + step
+
+        @pl.when(origin < peers)
+        def _():
+            for i, (ref, out) in enumerate(zip(sent, outs)):
+                pltpu.make_async_remote_copy(
+                    src_ref=ref.at[origin],
+                    dst_ref=out.at[origin],
+                    send_sem=send_sem.at[i, origin],
+                    recv_sem=recv_sem.at[i, origin],
+                    device_id={"ctx": origin},
+                    device_id_type=pl.DeviceIdType.MESH,
+                ).wait_recv()
+
+            def slot_head(head, inner):
+                at = pl.ds(pl.multiple_of(head * hd, hd), hd)
+                key_at = pl.ds(pl.multiple_of(head // local * hd, hd), hd)
+                live = stat_out[origin, pl.ds(2 * heads, 1), :] > 0
+                lse2 = jnp.where(live, stat_out[origin, pl.ds(head, 1), :] * LOG2E, DEAD)
+                delta = stat_out[origin, pl.ds(heads + head, 1), :]
+                dq, dk, dv = piece(
+                    k_ref[:, key_at], kt_ref[key_at, :], v_ref[:, key_at],
+                    q_out[origin, :, at], g_out[origin, :, at], lse2, delta, scale,
+                )
+                dk_ref[:, at] += dk
+                dv_ref[:, at] += dv
+                slot_ref[origin, :, at] = (dq.T * scale).astype(slot_ref.dtype)
+                return inner
+
+            lax.fori_loop(0, heads, slot_head, 0)
+
+        return carry
+
+    lax.fori_loop(1, peers, one_slot, 0)
+    for head in range(heads):
+        at = slice(head * hd, head * hd + hd)
+        dk_out[head] = (dk_ref[:, at] * scale).astype(dk_out.dtype)
+        dv_out[head] = dv_ref[:, at].astype(dv_out.dtype)
+    start_ctx("sends", me, peers, -1, sent, outs, send_sem, recv_sem)
 
 
 def return_kernel(
@@ -270,13 +288,22 @@
     anywhere = pl.BlockSpec(memory_space=pl.ANY)
     dma = lambda *shape: pltpu.SemaphoreType.DMA(shape)
     like = lambda *arrays: [jax.ShapeDtypeStruct(x.shape, x.dtype) for x in arrays]
-    own_shape = [jax.ShapeDtypeStruct((rows, width), f32)] * 3
-    got_q, got_g, got_stat, own_q, own_k, own_v = pl.pallas_call(
+    grads = jax.ShapeDtypeStruct((heads, rows, hd), bf16)
+    _, _, _, own_q, dq_out, dk, dv = pl.pallas_call(
         functools.partial(send_kernel, peers, scale),
         in_specs=[anywhere] * 3 + [vmem] * 6,
-        out_specs=[anywhere] * 3 + [vmem] * 3,
-        out_shape=like(q_blocks, g_blocks, send_stat) + own_shape,
-        scratch_shapes=[dma(3, peers), dma(3, peers)],
+        out_specs=[vmem] * 7,
+        out_shape=like(q_blocks, g_blocks, send_stat)
+        + [jax.ShapeDtypeStruct((rows, width), f32)]
+        + like(q_blocks)
+        + [grads, grads],
+        scratch_shapes=[
+            pltpu.VMEM((rows, width), f32),
+            pltpu.VMEM((rows, width), f32),
+            pltpu.VMEM((kv * hd, rows), bf16),
+            dma(3, peers),
+            dma(3, peers),
+        ],
         compiler_params=pltpu.CompilerParams(
             collective_id=0, has_side_effects=True, vmem_limit_bytes=VMEM_LIMIT
         ),
@@ -285,42 +312,8 @@
         q_blocks, g_blocks, send_stat, q2, g2, k2, v2,
         lse.reshape(heads, 1, rows), delta.reshape(heads, 1, rows),
     )
-    got_q = got_q.reshape(peers * QB, width)
-    got_g = got_g.reshape(peers * QB, width)
-
-    column = lambda n: pl.BlockSpec((n, hd), lambda h, *_: (0, h))
-    keys = pl.BlockSpec((rows, hd), lambda h, *_: (0, h // local))
-
-    marks = ((got_stat[:, 2 * heads, 0] > 0) & (peer_ids > device)).astype(jnp.int32)
-    stacked = pl.BlockSpec((1, rows, hd), lambda h, *_: (h, 0, 0))
-    dq_out, dk, dv = pl.pallas_call(
-        functools.partial(slots_kernel, scale),
-        grid_spec=pltpu.PrefetchScalarGridSpec(
-            num_scalar_prefetch=1,
-            grid=(heads,),
-            in_specs=[
-                column(peers * QB),
-                column(peers * QB),
-                pl.BlockSpec(got_stat.shape, lambda h, *_: (0, 0, 0)),
-                keys,
-                keys,
-                column(rows),
-                column(rows),
-            ],
-            out_specs=[column(peers * QB), stacked, stacked],
-            scratch_shapes=[pltpu.VMEM((rows, hd), f32)] * 2,
-        ),
-        out_shape=[
-            jax.ShapeDtypeStruct((peers * QB, width), bf16),
-            jax.ShapeDtypeStruct((heads, rows, hd), bf16),
-            jax.ShapeDtypeStruct((heads, rows, hd), bf16),
-        ],
-        compiler_params=params,
-        name="slots",
-    )(marks, got_q, got_g, got_stat, k2, v2, own_k, own_v)
 
     shards = lax.axis_size("head")
-    dq_out = dq_out.reshape(peers, QB, width)
     dk = dk.reshape(shards, heads // shards, rows, hd)
     dv = dv.reshape(shards, heads // shards, rows, hd)
     back, dk, dv = pl.pallas_call(

time: 123 us -> 114 us (0.927)
  Pallas kernels: 106 us -> 96.2 us
    pallas_call x1 -> x0, Pallas kernels: 20.5 us -> none  [body(): pl.pallas_call(functools.partial(slots_kernel, scale), grid_spec=pltpu.Pr...]
    pallas_call x1, Pallas kernels: 56.4 us -> 67.5 us  [body(): pl.pallas_call(functools.partial(send_kernel, peers, scale), in_specs=[an...]
    unnamed x28 -> x32, local copies, waits for them, and re-layouts: 5.48 us -> 5.47 us
where the time goes in v4:
time: 114 us
  Pallas kernels  96.2 us (84%)
  local copies, waits for them, and re-layouts  11.9 us (10%)
  other arithmetic  4.78 us (4%)
    pallas_call x1, Pallas kernels, body(): pl.pallas_call(functools.partial(send_kernel, peers, scale), in_specs=[an...  67.5 us
    pallas_call x1, Pallas kernels, body(): pl.pallas_call(functools.partial(return_kernel, peers, shards), in_specs=...  27 us
    unnamed x32, local copies, waits for them, and re-layouts  5.47 us
    reduce_sum x1, other arithmetic, body(): jnp.sum((out_grad.astype(f32) * outputs.astype(f32)).reshape(rows, heads,...  2.81 us

profile of v4, /device:TPU:1, one launch (start us, length us, event | category | flops | bytes accessed | tf_op | source)
XLA Modules:
  0.0 113.7 jit_solution(2257231571866509076)
XLA Ops:
  0.6 0.0 copy-start.7
  0.6 0.0 copy-start.9
  0.7 0.8 slice.11
  1.4 0.1 fusion
  1.6 2.8 %multiply_reduce_fusion = f32[1024,4]{1,0:T(8,128)S(1)} fusion(bf16[1024,4,1,128]{3,1,2,0:T(4,128)(2,1)} %param.11, bf16[1024,4,1,128]{3,1,2,0:T(4,128)(2,1)} %param.10), kind=kLoop, calls=%fused_computation | loop fusion | flops 2093056 | bytes 2113536 | tf_op jit(solution)/shard_map/reduce_sum | solution.py:259
  4.4 0.2 copy.22
  4.6 0.4 reshape_reshape.6.q_ref
  5.1 0.4 reshape_reshape.7.g_ref
  5.5 0.0 copy-start.13
  5.5 0.0 copy-start.14
  5.6 0.7 pick.1
  6.3 0.0 copy-start.1
  6.3 0.0 copy-start.2
  6.3 0.5 copy-done.13
  6.8 0.3 copy-done.14
  7.1 1.7 %copy_bitcast_fusion = (bf16[1024,512]{1,0:T(8,128)(2,1)}, bf16[1024,512]{1,0:T(8,128)(2,1)}) fusion(bf16[128,8,4,128]{3,2,1,0:T(4,128)(2,1)S(1)} %bitcast.43, bf16[128,8,4,128]{3,2,1,0:T(4,128)(2,1)S(1)} %bitcast.44), kind=kLoop, calls=%fused_computation.1 | loop fusion | bytes 4194304 | tf_op jit(solution)/shard_map/reshape | solution.py:256
  8.8 0.0 copy-done.10
  8.8 1.8 %copy_bitcast_fusion.2 = (bf16[1024,512]{1,0:T(8,128)(2,1)}, bf16[1024,512]{1,0:T(8,128)(2,1)}) fusion(bf16[128,8,4,128]{3,2,1,0:T(4,128)(2,1)S(1)} %bitcast.40, bf16[128,8,4,128]{3,2,1,0:T(4,128)(2,1)S(1)} %bitcast.41), kind=kLoop, calls=%fused_computation.3 | loop fusion | bytes 4194304 | tf_op jit(solution)/shard_map/reshape | solution.py:254
  10.6 67.5 %send.1 = (bf16[8,128,512]{2,1,0:T(8,128)(2,1)}, bf16[8,128,512]{2,1,0:T(8,128)(2,1)}, f32[8,12,128]{2,1,0:T(8,128)}, f32[1024,512]{1,0:T(8,128)}, bf16[8,128,51...) custom-call(bf16[8,128,512]{2,1,0:T(8,128)(2,1)} %copy-done.1, ...), custom_call_target="tpu_custom_call" | custom-call | tf_op jit(solution)/shard_map/send/pallas_call | solution.py:292
  78.1 0.0 copy-start.3
  78.1 1.0 copy-done.3
  79.1 1.0 copy-done.4
  80.1 1.0 copy-done.5
  81.1 27.0 %give_back.1 = (bf16[8,128,512]{2,1,0:T(8,128)(2,1)}, bf16[4,1,1024,128]{3,2,1,0:T(8,128)(2,1)}, bf16[4,1,1024,128]{3,2,1,0:T(8,128)(2,1)}) custom-call(bf16[8,128,512]{2,1,0:T(8,128)(2,1)} %copy-done.3, bf16[4,1,1024,128]{3,2,1,0:T(8,128)(2,1)} %bitcast.37, bf16[4,1,1024,128]{3,2,1,0:T(8,128)(2,1)} %bitcast.38), custom_call_target="tpu_custom_call" | custom-call | tf_op jit(solution)/shard_map/give_back/pallas_call | solution.py:319
  108.1 0.0 copy-done
  108.1 0.0 copy-start.6
  108.1 1.2 %copy-done.6 = bf16[8,128,512]{2,1,0:T(8,128)(2,1)S(1)} copy-done((bf16[8,128,512]{2,1,0:T(8,128)(2,1)S(1)}, bf16[8,128,512]{2,1,0:T(8,128)(2,1)}, u32[]{:S(2)}) %copy-start.6) | copy-done | bytes 1048600
  109.3 1.0 merge.1
  110.3 1.1 reshape.80
  111.5 0.4 copy-done.12
  111.9 0.9 reduce_sum.45
  112.8 0.9 reduce_sum.44
  (23 shorter events, 0.1 us)
Async XLA Ops:
  0.6 4.0 %copy-start.7 = (f32[4,1,1024]{2,1,0:T(1,128)S(1)}, f32[4,1,1024]{2,1,0:T(1,128)}, u32[]{:S(2)}) copy-start(f32[4,1,1024]{2,1,0:T(1,128)} %lse_ref.1) | copy-start | bytes 49156
  0.6 4.0 %copy-start.9 = (bf16[1024,4,1,128]{3,1,2,0:T(4,128)(2,1)S(1)}, bf16[1024,4,1,128]{3,1,2,0:T(4,128)(2,1)}, u32[]{:S(2)}) copy-start(bf16[1024,4,1,128]{3,1,2,0:T(4,128)(2,1)} %param.7) | copy-start | bytes 3145732
  1.6 3.5 %copy-start.8 = (bf16[1024,4,1,128]{3,1,2,0:T(4,128)(2,1)S(1)}, bf16[1024,4,1,128]{3,1,2,0:T(4,128)(2,1)}, u32[]{:S(2)}) copy-start(bf16[1024,4,1,128]{3,1,2,0:T(4,128)(2,1)} %param.10) | copy-start | bytes 3145732
  5.5 1.2 %copy-start.13 = (bf16[1024,4,128]{2,1,0:T(4,128)(2,1)S(1)}, bf16[1024,4,128]{2,1,0:T(4,128)(2,1)}, u32[]{:S(2)}) copy-start(bf16[1024,4,128]{2,1,0:T(4,128)(2,1)} %param.9) | copy-start | bytes 3145732
  5.5 1.5 %copy-start.14 = (bf16[1024,4,128]{2,1,0:T(4,128)(2,1)S(1)}, bf16[1024,4,128]{2,1,0:T(4,128)(2,1)}, u32[]{:S(2)}) copy-start(bf16[1024,4,128]{2,1,0:T(4,128)(2,1)} %param.8) | copy-start | bytes 3145732
  6.3 2.5 %copy-start.1 = (bf16[8,128,512]{2,1,0:T(8,128)(2,1)}, bf16[8,128,512]{2,1,0:T(8,128)(2,1)S(1)}, u32[]{:S(2)}) copy-start(bf16[8,128,512]{2,1,0:T(8,128)(2,1)S(1)} %get-tuple-element.13.q_ref) | copy-start | bytes 3145732
  6.3 2.5 %copy-start.2 = (bf16[8,128,512]{2,1,0:T(8,128)(2,1)}, bf16[8,128,512]{2,1,0:T(8,128)(2,1)S(1)}, u32[]{:S(2)}) copy-start(bf16[8,128,512]{2,1,0:T(8,128)(2,1)S(1)} %get-tuple-element.14.g_ref) | copy-start | bytes 3145732
  7.1 1.7 %copy-start.10 = (bf16[1024,4,1,128]{3,1,2,0:T(4,128)(2,1)S(1)}, bf16[1024,4,1,128]{3,1,2,0:T(4,128)(2,1)}, u32[]{:S(2)}) copy-start(bf16[1024,4,1,128]{3,1,2,0:T(4,128)(2,1)} %param.7) | copy-start | bytes 3145732
  78.1 1.0 copy-start.3
  79.1 1.0 copy-start.4
  80.1 1.0 copy-start.5
  81.1 27.0 %copy-start.15 = (s32[8,3]{0,1:T(4,128)S(1)}, s32[8,3]{0,1:T(4,128)}, u32[]{:S(2)}) copy-start(s32[8,3]{0,1:T(4,128)} %param.13) | copy-start | bytes 292
  81.1 27.0 %copy-start = (f32[1024,512]{1,0:T(8,128)S(1)}, f32[1024,512]{1,0:T(8,128)}, u32[]{:S(2)}) copy-start(f32[1024,512]{1,0:T(8,128)} %get-tuple-element.16.own_ref) | copy-start | bytes 6291460
  108.1 1.2 %copy-start.6 = (bf16[8,128,512]{2,1,0:T(8,128)(2,1)S(1)}, bf16[8,128,512]{2,1,0:T(8,128)(2,1)}, u32[]{:S(2)}) copy-start(bf16[8,128,512]{2,1,0:T(8,128)(2,1)} %get-tuple-element.20.back_ref) | copy-start | bytes 3145732
  110.3 1.6 %copy-start.12 = (bf16[4,1,1024,128]{3,2,1,0:T(8,128)(2,1)S(1)}, bf16[4,1,1024,128]{3,2,1,0:T(8,128)(2,1)}, u32[]{:S(2)}) copy-start(bf16[4,1,1024,128]{3,2,1,0:T(8,128)(2,1)} %get-tuple-element.22) | copy-start | bytes 3145732
  110.3 2.5 %copy-start.11 = (bf16[4,1,1024,128]{3,2,1,0:T(8,128)(2,1)S(1)}, bf16[4,1,1024,128]{3,2,1,0:T(8,128)(2,1)}, u32[]{:S(2)}) copy-start(bf16[4,1,1024,128]{3,2,1,0:T(8,128)(2,1)} %get-tuple-element.21) | copy-start | bytes 3145732
